TPU v7x, 32 devices: a whole 2x2x4 slice. The times are simulated.
32 devices in a mesh: fsdp: 16 (over z, y, core), tp: 2 (over x).
Axes of the slice: x: 2, y: 2, z: 4, core: 2. Of those that a mesh axis runs over, the one named last changes fastest.
Arguments:
- tokens_in: bfloat16 [256, 196, 768], P(('fsdp', 'tp')), may hold values from -6 to 6
- out_grad: bfloat16 [256, 196, 768], P(('fsdp', 'tp')), may hold values from -6 to 6
- image_counts: int32 [16], P('fsdp'), may hold values from 1 to 16, 192 in all
- norm_params: float32 [4, 768], replicated, may hold values from -0.9 to 1.9, as said below
- w_qkv: float32 [3, 768, 768], P(None, 'fsdp', 'tp'), may hold values from -0.21875 to 0.21875
- bias_qv: float32 [2, 768], P(None, ('tp', 'fsdp')), may hold values from -3 to 3
- w_out: float32 [768, 768], P('tp', 'fsdp'), may hold values from -2.5 to 2.5
- w_fc1: float32 [768, 3072], P('fsdp', 'tp'), may hold values from -0.21875 to 0.21875
- bias_fc1: float32 [3072], P(('tp', 'fsdp')), may hold values from -3 to 3
- w_fc2: float32 [3072, 768], P('tp', 'fsdp'), may hold values from -0.109375 to 0.109375
- bias_out: float32 [2, 768], replicated, may hold values from -3 to 3
- first_norm: float32 [4, 768], replicated, may hold values from -1976.7312 to 1976.7312
- first_qkv: float32 [3, 768, 768], P(None, 'fsdp', 'tp'), may hold values from -593.01935 to 593.01935
- first_bias_qv: float32 [2, 768], P(None, ('tp', 'fsdp')), may hold values from -1976.7312 to 1976.7312
- first_out: float32 [768, 768], P('tp', 'fsdp'), may hold values from -94.08 to 94.08
- first_fc1: float32 [768, 3072], P('fsdp', 'tp'), may hold values from -60.48 to 60.48
- first_bias_fc1: float32 [3072], P(('tp', 'fsdp')), may hold values from -60.48 to 60.48
- first_fc2: float32 [3072, 768], P('tp', 'fsdp'), may hold values from -107.52 to 107.52
- first_bias_out: float32 [2, 768], replicated, may hold values from -174.72 to 174.72
- second_norm: float32 [4, 768], replicated, may hold values from 1477.1814 to 14771.814
- second_qkv: float32 [3, 768, 768], P(None, 'fsdp', 'tp'), may hold values from 134.8731 to 1348.7308
- second_bias_qv: float32 [2, 768], P(None, ('tp', 'fsdp')), may hold values from 1477.1814 to 14771.814
- second_out: float32 [768, 768], P('tp', 'fsdp'), may hold values from 3.01056 to 30.1056
- second_fc1: float32 [768, 3072], P('fsdp', 'tp'), may hold values from 1.354752 to 13.54752
- second_bias_fc1: float32 [3072], P(('tp', 'fsdp')), may hold values from 1.354752 to 13.54752
- second_fc2: float32 [3072, 768], P('tp', 'fsdp'), may hold values from 4.51584 to 45.1584
- second_bias_out: float32 [2, 768], replicated, may hold values from 12.04224 to 120.4224
Outputs:
- block_out: bfloat16 [256, 196, 768], P(('fsdp', 'tp'))
- grad_tokens: float32 [256, 196, 768], P(('fsdp', 'tp'))
- grad_norm: float32 [4, 768], replicated
- grad_qkv: float32 [3, 768, 768], P(None, 'fsdp', 'tp')
- grad_bias_qv: float32 [2, 768], P(None, ('tp', 'fsdp'))
- grad_out: float32 [768, 768], P('tp', 'fsdp')
- grad_fc1: float32 [768, 3072], P('fsdp', 'tp')
- grad_bias_fc1: float32 [3072], P(('tp', 'fsdp'))
- grad_fc2: float32 [3072, 768], P('tp', 'fsdp')
- grad_bias_out: float32 [2, 768], replicated
- step_norm: float32 [4, 768], replicated
- new_qkv: float32 [3, 768, 768], P(None, 'fsdp', 'tp')
- step_bias_qv: float32 [2, 768], P(None, ('tp', 'fsdp'))
- step_out: float32 [768, 768], P('tp', 'fsdp')
- new_fc1: float32 [768, 3072], P('fsdp', 'tp')
- step_bias_fc1: float32 [3072], P(('tp', 'fsdp'))
- new_fc2: float32 [3072, 768], P('tp', 'fsdp')
- step_bias_out: float32 [2, 768], replicated
- new_first_norm: float32 [4, 768], replicated
- new_first_qkv: float32 [3, 768, 768], P(None, 'fsdp', 'tp')
- new_first_bias_qv: float32 [2, 768], P(None, ('tp', 'fsdp'))
- new_first_out: float32 [768, 768], P('tp', 'fsdp')
- new_first_fc1: float32 [768, 3072], P('fsdp', 'tp')
- new_first_bias_fc1: float32 [3072], P(('tp', 'fsdp'))
- new_first_fc2: float32 [3072, 768], P('tp', 'fsdp')
- new_first_bias_out: float32 [2, 768], replicated
- new_second_norm: float32 [4, 768], replicated
- new_second_qkv: float32 [3, 768, 768], P(None, 'fsdp', 'tp')
- new_second_bias_qv: float32 [2, 768], P(None, ('tp', 'fsdp'))
- new_second_out: float32 [768, 768], P('tp', 'fsdp')
- new_second_fc1: float32 [768, 3072], P('fsdp', 'tp')
- new_second_bias_fc1: float32 [3072], P(('tp', 'fsdp'))
- new_second_fc2: float32 [3072, 768], P('tp', 'fsdp')
- new_second_bias_out: float32 [2, 768], replicated
Inputs may be any that keep to these rules, and one draw needn't show every extreme that they name: image_counts[g] live images fill slots 0 to image_counts[g] - 1 of group g; at least one group is full. `norm_params`: rows 0 and 2 are gains, rows 1 and 3 shifts.
All inputs are finite; a program needn't handle non-finite values.
Results may differ from a plain program's by a relative error of at most 0.013.
Values may be sent and summed in bfloat16 or wider, within the bound.
A program may use at most 320 MiB of HBM per device.

v0:
```python
import jax
import jax.numpy as jnp
from jax import lax
from jax.sharding import PartitionSpec as P

HEAD_DIM = 64
ADAM_STEP = 10


norm_eps = 1e-06
learn_rate = 0.02
beta_one = 0.9
beta_two = 0.999
adam_eps = 1e-08
decay_rate = 0.05


def layer_norm(rows_in, gain_vec, shift_vec):
    centre = rows_in - jnp.mean(rows_in, axis=-1, keepdims=True)
    spread = jnp.mean(centre * centre, axis=-1, keepdims=True)
    return centre * lax.rsqrt(spread + norm_eps) * gain_vec + shift_vec


def exact_gelu(rows_in):
    return jax.nn.gelu(rows_in, approximate=False)


def adamw(parameter, gradient, moment_one, moment_two, decay_on):
    one_new = beta_one * moment_one + (1.0 - beta_one) * gradient
    two_new = beta_two * moment_two + (1.0 - beta_two) * gradient * gradient
    one_hat = one_new / (1.0 - beta_one**ADAM_STEP)
    two_hat = two_new / (1.0 - beta_two**ADAM_STEP)
    update = one_hat / (jnp.sqrt(two_hat) + adam_eps) + decay_on * parameter
    return (-learn_rate * update, one_new, two_new)


def per_device(
    tokens_in,
    out_grad,
    image_counts,
    norm_params,
    w_qkv,
    bias_qv,
    w_out,
    w_fc1,
    bias_fc1,
    w_fc2,
    bias_out,
    first_norm,
    first_qkv,
    first_bias_qv,
    first_out,
    first_fc1,
    first_bias_fc1,
    first_fc2,
    first_bias_out,
    second_norm,
    second_qkv,
    second_bias_qv,
    second_out,
    second_fc1,
    second_bias_fc1,
    second_fc2,
    second_bias_out,
):
    images = tokens_in.shape[0]
    seq_len = tokens_in.shape[1]
    score_scale = HEAD_DIM ** (-0.5)
    inputs = tokens_in.astype(jnp.float32)
    slot_ids = lax.axis_index("tp") * images + jnp.arange(images)
    live_mask = (slot_ids < image_counts[0]).astype(jnp.float32)
    live_grad = out_grad.astype(jnp.float32) * live_mask[:, None, None]
    qkv_all, bqv_all, wout_all = (
        lax.all_gather(w_qkv.astype(jnp.bfloat16), "fsdp", axis=1, tiled=True),
        lax.all_gather(bias_qv.astype(jnp.bfloat16), "fsdp", axis=1, tiled=True),
        lax.all_gather(w_out.astype(jnp.bfloat16), "fsdp", axis=1, tiled=True),
    )
    fc1_all, bfc1_all, fc2_all = (
        lax.all_gather(w_fc1.astype(jnp.bfloat16), "fsdp", axis=0, tiled=True),
        lax.all_gather(bias_fc1.astype(jnp.bfloat16), "fsdp", axis=0, tiled=True),
        lax.all_gather(w_fc2.astype(jnp.bfloat16), "fsdp", axis=1, tiled=True),
    )
    hidden_one = layer_norm(inputs, norm_params[0], norm_params[1]).astype(jnp.bfloat16)
    qkv_use, bqv_use, wout_use = (
        lax.all_gather(qkv_all, "tp", axis=2, tiled=True),
        lax.all_gather(bqv_all, "tp", axis=1, tiled=True),
        lax.all_gather(wout_all, "tp", axis=0, tiled=True),
    )
    group_images = hidden_one.shape[0]
    projected = jnp.einsum("gsd,cdf->cgsf", hidden_one, qkv_use, preferred_element_type=jnp.float32)
    width_local = projected.shape[3]
    shape_heads = (group_images, seq_len, width_local // HEAD_DIM, HEAD_DIM)
    queries = (projected[0] + bqv_use[0]).astype(jnp.bfloat16).reshape(shape_heads)
    key_vecs = projected[1].astype(jnp.bfloat16).reshape(shape_heads)
    value_vecs = (projected[2] + bqv_use[1]).astype(jnp.bfloat16).reshape(shape_heads)
    scores = (
        jnp.einsum("gqhe,gkhe->ghqk", queries, key_vecs, preferred_element_type=jnp.float32)
        * score_scale
    )
    log_total = jax.nn.logsumexp(scores, axis=-1, keepdims=True)
    probs_low = jnp.exp(scores - log_total).astype(jnp.bfloat16)
    context = jnp.einsum(
        "ghqk,gkhe->gqhe", probs_low, value_vecs, preferred_element_type=jnp.float32
    )
    context = context.astype(jnp.bfloat16).reshape(group_images, seq_len, width_local)
    attn_part = jnp.einsum("gsf,fd->gsd", context, wout_use, preferred_element_type=jnp.float32)
    middle = inputs + attn_part + bias_out[0]
    hidden_two = layer_norm(middle, norm_params[2], norm_params[3]).astype(jnp.bfloat16)
    mlp_in = lax.all_gather(hidden_two, "tp", axis=0, tiled=True)
    fc1_use, bfc1_use, fc2_use = (fc1_all, bfc1_all, fc2_all)
    pre_act = (
        jnp.einsum("gsd,df->gsf", mlp_in, fc1_use, preferred_element_type=jnp.float32) + bfc1_use
    )
    activated = exact_gelu(pre_act).astype(jnp.bfloat16)
    mlp_part = jnp.einsum("gsf,fd->gsd", activated, fc2_use, preferred_element_type=jnp.float32)
    mlp_sum = lax.psum_scatter(
        mlp_part.astype(jnp.bfloat16), "tp", scatter_dimension=0, tiled=True
    ).astype(jnp.float32)
    block_out = (middle + mlp_sum + bias_out[1]).astype(jnp.bfloat16)
    grad_mlp = live_grad.astype(jnp.bfloat16)
    grad_mlp_in = lax.all_gather(grad_mlp, "tp", axis=0, tiled=True)
    grad_w2 = jnp.einsum("gsf,gsd->fd", activated, grad_mlp_in, preferred_element_type=jnp.float32)
    grad_act = jnp.einsum("gsd,fd->gsf", grad_mlp_in, fc2_use, preferred_element_type=jnp.float32)
    gelu_out, gelu_pull = jax.vjp(exact_gelu, pre_act)
    grad_pre = gelu_pull(grad_act)[0].astype(jnp.bfloat16)
    grad_b1 = jnp.sum(grad_pre.astype(jnp.float32), axis=(0, 1))
    grad_w1 = jnp.einsum("gsd,gsf->df", mlp_in, grad_pre, preferred_element_type=jnp.float32)
    grad_h2_part = jnp.einsum("gsf,df->gsd", grad_pre, fc1_use, preferred_element_type=jnp.float32)
    grad_h2 = lax.psum_scatter(
        grad_h2_part.astype(jnp.bfloat16), "tp", scatter_dimension=0, tiled=True
    ).astype(jnp.float32)
    norm_two, norm_two_pull = jax.vjp(layer_norm, middle, norm_params[2], norm_params[3])
    grad_mid_ln, grad_gain_two, grad_shift_two = norm_two_pull(grad_h2)
    grad_middle = live_grad + grad_mid_ln
    grad_attn = grad_middle.astype(jnp.bfloat16)
    grad_wo = jnp.einsum("gsf,gsd->fd", context, grad_attn, preferred_element_type=jnp.float32)
    grad_ctx = jnp.einsum("gsd,fd->gsf", grad_attn, wout_use, preferred_element_type=jnp.float32)
    grad_ctx = grad_ctx.astype(jnp.bfloat16).reshape(shape_heads)
    scores_again = (
        jnp.einsum("gqhe,gkhe->ghqk", queries, key_vecs, preferred_element_type=jnp.float32)
        * score_scale
    )
    probs_again = jnp.exp(scores_again - log_total)
    grad_probs = jnp.einsum(
        "gqhe,gkhe->ghqk", grad_ctx, value_vecs, preferred_element_type=jnp.float32
    )
    row_terms = jnp.sum(probs_again * grad_probs, axis=-1, keepdims=True)
    grad_scores = (probs_again * (grad_probs - row_terms)).astype(jnp.bfloat16)
    grad_query = (
        jnp.einsum("ghqk,gkhe->gqhe", grad_scores, key_vecs, preferred_element_type=jnp.float32)
        * score_scale
    ).astype(jnp.bfloat16)
    grad_keys = (
        jnp.einsum("ghqk,gqhe->gkhe", grad_scores, queries, preferred_element_type=jnp.float32)
        * score_scale
    ).astype(jnp.bfloat16)
    grad_values = jnp.einsum(
        "ghqk,gqhe->gkhe",
        probs_again.astype(jnp.bfloat16),
        grad_ctx,
        preferred_element_type=jnp.float32,
    ).astype(jnp.bfloat16)
    grad_proj = jnp.stack([grad_query, grad_keys, grad_values]).reshape(
        3, group_images, seq_len, width_local
    )
    grad_bqv = jnp.stack(
        [
            jnp.sum(grad_proj[0].astype(jnp.float32), axis=(0, 1)),
            jnp.sum(grad_proj[2].astype(jnp.float32), axis=(0, 1)),
        ]
    )
    grad_wqkv = jnp.einsum(
        "gsd,cgsf->cdf", hidden_one, grad_proj, preferred_element_type=jnp.float32
    )
    grad_h1_part = jnp.einsum(
        "cgsf,cdf->gsd", grad_proj, qkv_use, preferred_element_type=jnp.float32
    )
    grad_wqkv, grad_bqv, grad_wo = (
        lax.psum_scatter(
            grad_wqkv.astype(jnp.bfloat16), "tp", scatter_dimension=2, tiled=True
        ).astype(jnp.float32),
        lax.psum_scatter(
            grad_bqv.astype(jnp.bfloat16), "tp", scatter_dimension=1, tiled=True
        ).astype(jnp.float32),
        lax.psum_scatter(
            grad_wo.astype(jnp.bfloat16), "tp", scatter_dimension=0, tiled=True
        ).astype(jnp.float32),
    )
    norm_one, norm_one_pull = jax.vjp(layer_norm, inputs, norm_params[0], norm_params[1])
    grad_in_ln, grad_gain_one, grad_shift_one = norm_one_pull(grad_h1_part)
    grad_tokens = grad_middle + grad_in_ln
    g_qkv, g_bqv, g_out, g_fc1, g_bfc1, g_fc2 = (
        lax.psum_scatter(grad_wqkv, "fsdp", scatter_dimension=1, tiled=True),
        lax.psum_scatter(grad_bqv, "fsdp", scatter_dimension=1, tiled=True),
        lax.psum_scatter(grad_wo, "fsdp", scatter_dimension=1, tiled=True),
        lax.psum_scatter(grad_w1, "fsdp", scatter_dimension=0, tiled=True),
        lax.psum_scatter(grad_b1, "fsdp", scatter_dimension=0, tiled=True),
        lax.psum_scatter(grad_w2, "fsdp", scatter_dimension=1, tiled=True),
    )
    norm_terms = jnp.stack([grad_gain_one, grad_shift_one, grad_gain_two, grad_shift_two])
    bias_terms = jnp.stack([jnp.sum(grad_middle, axis=(0, 1)), jnp.sum(live_grad, axis=(0, 1))])
    g_norm, g_bout = lax.psum((norm_terms, bias_terms), ("fsdp", "tp"))
    s_norm, a_norm, b_norm = adamw(norm_params, g_norm, first_norm, second_norm, 0.0)
    s_qkv, a_qkv, b_qkv = adamw(w_qkv, g_qkv, first_qkv, second_qkv, decay_rate)
    s_bqv, a_bqv, b_bqv = adamw(bias_qv, g_bqv, first_bias_qv, second_bias_qv, 0.0)
    s_out, a_out, b_out = adamw(w_out, g_out, first_out, second_out, decay_rate)
    s_fc1, a_fc1, b_fc1 = adamw(w_fc1, g_fc1, first_fc1, second_fc1, decay_rate)
    s_bfc1, a_bfc1, b_bfc1 = adamw(bias_fc1, g_bfc1, first_bias_fc1, second_bias_fc1, 0.0)
    s_fc2, a_fc2, b_fc2 = adamw(w_fc2, g_fc2, first_fc2, second_fc2, decay_rate)
    s_bout, a_bout, b_bout = adamw(bias_out, g_bout, first_bias_out, second_bias_out, 0.0)
    return (
        block_out,
        grad_tokens,
        g_norm,
        g_qkv,
        g_bqv,
        g_out,
        g_fc1,
        g_bfc1,
        g_fc2,
        g_bout,
        s_norm,
        w_qkv + s_qkv,
        s_bqv,
        s_out,
        w_fc1 + s_fc1,
        s_bfc1,
        w_fc2 + s_fc2,
        s_bout,
        a_norm,
        a_qkv,
        a_bqv,
        a_out,
        a_fc1,
        a_bfc1,
        a_fc2,
        a_bout,
        b_norm,
        b_qkv,
        b_bqv,
        b_out,
        b_fc1,
        b_bfc1,
        b_fc2,
        b_bout,
    )


def solution(mesh):
    placed = (
        P(("fsdp", "tp"), None, None),
        P(("fsdp", "tp"), None, None),
        P("fsdp"),
        P(),
        P(None, "fsdp", "tp"),
        P(None, ("tp", "fsdp")),
        P("tp", "fsdp"),
        P("fsdp", "tp"),
        P(("tp", "fsdp")),
        P("tp", "fsdp"),
        P(),
        P(),
        P(None, "fsdp", "tp"),
        P(None, ("tp", "fsdp")),
        P("tp", "fsdp"),
        P("fsdp", "tp"),
        P(("tp", "fsdp")),
        P("tp", "fsdp"),
        P(),
        P(),
        P(None, "fsdp", "tp"),
        P(None, ("tp", "fsdp")),
        P("tp", "fsdp"),
        P("fsdp", "tp"),
        P(("tp", "fsdp")),
        P("tp", "fsdp"),
        P(),
    )
    return jax.shard_map(
        per_device,
        mesh=mesh,
        in_specs=placed,
        out_specs=(
            P(("fsdp", "tp"), None, None),
            P(("fsdp", "tp"), None, None),
            P(),
            P(None, "fsdp", "tp"),
            P(None, ("tp", "fsdp")),
            P("tp", "fsdp"),
            P("fsdp", "tp"),
            P(("tp", "fsdp")),
            P("tp", "fsdp"),
            P(),
            P(),
            P(None, "fsdp", "tp"),
            P(None, ("tp", "fsdp")),
            P("tp", "fsdp"),
            P("fsdp", "tp"),
            P(("tp", "fsdp")),
            P("tp", "fsdp"),
            P(),
            P(),
            P(None, "fsdp", "tp"),
            P(None, ("tp", "fsdp")),
            P("tp", "fsdp"),
            P("fsdp", "tp"),
            P(("tp", "fsdp")),
            P("tp", "fsdp"),
            P(),
            P(),
            P(None, "fsdp", "tp"),
            P(None, ("tp", "fsdp")),
            P("tp", "fsdp"),
            P("fsdp", "tp"),
            P(("tp", "fsdp")),
            P("tp", "fsdp"),
            P(),
        ),
        check_vma=False,
    )
```

profile of v0, /device:TPU:0, one launch (start us, length us, event | category | flops | bytes accessed | tf_op | source)
XLA Modules:
  0.0 998.2 jit_solution(17113093099460672231)
XLA Ops:
  7.3 1.7 convert_element_type.168
  9.1 45.0 %all-gather.9.cloned.1.call-done = bf16[3,768,384]{2,1,0:T(8,128)(2,1)} async-done(((bf16[3,48,384]{2,1,0:T(8,128)(2,1)}), bf16[3,768,384]{2,1,0:T(8,128)(2,1)}) %all-gather.9.cloned.1.call-update) | async-done | bytes 1769488 | tf_op jit(solution)/shard_map/all_gather | solution.py:74
  55.1 20.9 %all_gather.37 = bf16[384,768]{0,1:T(8,128)(2,1)S(1)} all-gather(bf16[384,48]{0,1:T(8,128)(2,1)S(1)} %convert_element_type.180), channel_id=1, replica_groups=mesh['fsdp'=16,'tp'=2] {'fsdp'}, dimensions={1}, use_global_device_ids=true | all-gather | bytes 626688 | tf_op jit(solution)/shard_map/all_gather | solution.py:76
  80.3 17.3 %all-gather = bf16[16,24,2]{1,2,0:T(2,128)(2,1)S(1)} all-gather(bf16[1,24,2]{1,2,0:T(2,128)(2,1)S(1)} %convert_bitcast_fusion), channel_id=1, replica_groups=mesh['fsdp'=16,'tp'=2] {'fsdp'}, dimensions={0}, use_global_device_ids=true | all-gather | bytes 1632 | tf_op jit(solution)/shard_map/all_gather | solution.py:75
  97.8 4.3 all_gather.36
  102.9 1.1 all-gather.11.cloned.1.call-done
  104.0 11.9 %convolution_bitcast_fusion = f32[3,8,196,768]{3,2,0,1:T(8,128)} fusion(bf16[3,768,768]{2,1,0:T(8,128)(2,1)} %all-gather.11.cloned.1.call-done, f32[768]{0:T(1024)S(1)} %get-tuple-element.179, f32[768]{0:T(1024)S(1)} %get-tuple-element.180, f32[8,196]{1,0:T(8,128)S(1)} %fusion.68, f32[8,196]{1,0:T(8,128)S(1)} %broadcast_multiply_fusion.1, ...), kind=kOutput, calls=%fused_computation.33 | convolution fusion | flops 5556289536 | bytes 20416768 | tf_op jit(solution)/shard_map/gsd,cdf->cgsf/dot_general | solution.py:90
  115.9 8.4 fusion.89
  124.3 4.1 slice.69
  128.4 6.3 copy.176
  134.7 4.5 copy.177
  139.2 13.7 %multiply_reduce_fusion.1 = (f32[8,12,196]{2,1,0:T(8,128)S(1)}, f32[8,12,196,196]{2,3,1,0:T(8,128)}) fusion(bf16[8,196,12,64]{1,3,2,0:T(8,128)(2,1)} %bitcast.113, f32[8,196,12,64]{1,3,2,0:T(8,128)} %bitcast.111, f32[12,64]{1,0:T(8,128)S(1)} %reshape.215), kind=kOutput, calls=%fused_computation.27 | convolution fusion | flops 481821312 | bytes 22055424 | tf_op jit(solution)/shard_map/gqhe,gkhe->ghqk/dot_general | solution.py:97
  152.9 6.8 copy.174
  159.7 11.9 %exponential_reduce_fusion = f32[8,12,196]{2,1,0:T(8,128)S(1)} fusion(f32[8,12,196,196]{2,3,1,0:T(8,128)} %get-tuple-element.229, f32[8,12,196]{2,1,0:T(8,128)S(1)} %is-finite_select_fusion), kind=kLoop, calls=%fused_computation.25 | loop fusion | flops 11044992 | bytes 14902272 | tf_op jit(solution)/shard_map/reduce_sum | solution.py:100
  171.7 14.1 %convolution_convert_fusion.3 = bf16[8,12,64,196]{3,2,1,0:T(8,128)(2,1)} fusion(f32[8,12,196,196]{2,3,1,0:T(8,128)} %get-tuple-element.229, f32[8,12,196]{2,1,0:T(8,128)S(1)} %log_add_fusion, f32[8,196,12,64]{1,3,2,0:T(8,128)} %bitcast.109, f32[12,64]{1,0:T(8,128)S(1)} %reshape.214), kind=kOutput, calls=%fused_computation.97 | convolution fusion | flops 486732288 | bytes 22055424 | tf_op jit(solution)/shard_map/ghqk,gkhe->gqhe/dot_general | solution.py:102
  185.8 5.0 fusion.91
  193.8 1.9 copy.181
  197.2 1.9 copy.184
  200.7 33.1 %all-reduce = bf16[1536]{0:T(1024)(128)(2,1)S(1)} all-reduce(bf16[1536]{0:T(1024)(128)(2,1)S(1)} %dynamic-update-slice), channel_id=1, replica_groups=mesh['fsdp'=16,'tp'=2] {'fsdp'}, use_global_device_ids=true, to_apply=%add | all-reduce | flops 1536 | bytes 6144
  233.9 25.9 %all-gather.15.cloned.1.call-done = bf16[16,196,768]{2,0,1:T(8,128)(2,1)} async-done(((bf16[8,196,768]{2,0,1:T(8,128)(2,1)}), bf16[16,196,768]{2,0,1:T(8,128)(2,1)}) %all-gather.15.cloned.1.call-update) | async-done | bytes 4816912 | tf_op jit(solution)/shard_map/all_gather | solution.py:109
  259.8 17.4 %fusion.8 = (u16[196,1536]{1,0:T(8,128)(2,1)S(1)}, u16[196,1536]{1,0:T(8,128)(2,1)S(1)}, f32[16,196,1536]{2,1,0:T(8,128)S(1)}) fusion(f32[1536]{0:T(1024)S(1)} %convert_element_type.184, bf16[768,1536]{1,0:T(8,128)(2,1)} %all-gather.17.cloned.1.call-done, bf16[16,196,768]{2,0,1:T(8,128)(2,1)} %all-gather.15.cloned.1.call-done), kind=kOutput, calls=%fused_computation.30 | convolution fusion | flops 7465586688 | bytes 27654144 | tf_op jit(solution)/shard_map/gsd,df->gsf/dot_general | solution.py:112
  277.2 6.6 copy-done.6
  283.8 45.1 %multiply_convert_fusion.1 = (bf16[16,196,1536]{2,1,0:T(8,128)(2,1)}, f32[16,196,1536]{2,1,0:T(8,128)}) fusion(f32[16,196,1536]{2,1,0:T(8,128)S(1)} %get-tuple-element.232, u16[196,1536]{1,0:T(8,128)(2,1)S(1)} %get-tuple-element.171, u16[196,1536]{1,0:T(8,128)(2,1)S(1)} %get-tuple-element.170), kind=kLoop, calls=%fused_computation.11 | loop fusion | flops 337182720 | bytes 49373184 | tf_op jit(solution)/shard_map/convert_element_type | solution.py:114
  328.9 16.8 %fusion.36 = f32[1536,768]{0,1:T(8,128)} fusion(bf16[16,196,1536]{2,1,0:T(8,128)(2,1)} %get-tuple-element.219, bf16[16,196,768]{2,0,1:T(8,128)(2,1)} %all-gather.21.cloned.1.call-done), kind=kOutput, calls=%fused_computation.80 | convolution fusion | flops 7398752256 | bytes 19169280 | tf_op jit(solution)/shard_map/gsf,gsd->fd/dot_general | solution.py:122
  345.9 75.6 %reduce-scatter.24.cloned.1.call-done = f32[1536,48]{0,1:T(8,128)} async-done(((f32[1536,768]{0,1:T(8,128)}), f32[1536,48]{0,1:T(8,128)}) %reduce-scatter.24.cloned.1.call-update) | async-done | bytes 294928 | tf_op jit(solution)/shard_map/reduce_scatter | solution.py:198
  421.5 2.1 multiply_add_fusion
  423.7 42.2 %all-gather.19.cloned.1.call-done = bf16[1536,768]{0,1:T(8,128)(2,1)} async-done(((bf16[1536,48]{0,1:T(8,128)(2,1)}), bf16[1536,768]{0,1:T(8,128)(2,1)}) %all-gather.19.cloned.1.call-update) | async-done | bytes 2359312 | tf_op jit(solution)/shard_map/all_gather | solution.py:81
  465.9 29.5 %convert_reduce_fusion = (f32[1536]{0:T(1024)}, bf16[16,196,1536]{2,1,0:T(8,128)(2,1)}) fusion(f32[16,196,1536]{2,1,0:T(8,128)} %get-tuple-element.220, f32[16,196,1536]{2,1,0:T(8,128)} %copy-done.6, bf16[1536,768]{0,1:T(8,128)(2,1)} %all-gather.19.cloned.1.call-done, bf16[16,196,768]{2,0,1:T(8,128)(2,1)} %all-gather.21.cloned.1.call-done), kind=kOutput, calls=%fused_computation.7 | convolution fusion | flops 7475821056 | bytes 55351296 | tf_op jit(solution)/shard_map/gsd,fd->gsf/dot_general | solution.py:123
  495.4 13.5 %convolution_convert_fusion = bf16[16,196,768]{2,1,0:T(8,128)(2,1)} fusion(bf16[16,196,1536]{2,1,0:T(8,128)(2,1)} %get-tuple-element.242, bf16[768,1536]{1,0:T(8,128)(2,1)S(1)} %copy-done.71), kind=kOutput, calls=%fused_computation.88 | convolution fusion | flops 7401160704 | bytes 16809984 | tf_op jit(solution)/shard_map/gsf,df->gsd/dot_general | solution.py:128
  509.0 1.6 copy-done.72
  510.6 14.0 %convolution_convert_fusion.1 = bf16[16,196,768]{2,1,0:T(8,128)(2,1)} fusion(bf16[16,196,1536]{2,1,0:T(8,128)(2,1)} %get-tuple-element.219, bf16[1536,768]{0,1:T(8,128)(2,1)S(1)} %copy-done.72), kind=kOutput, calls=%fused_computation.89 | convolution fusion | flops 7401160704 | bytes 16809984 | tf_op jit(solution)/shard_map/gsf,fd->gsd/dot_general | solution.py:115
  524.7 14.1 %fusion.33 = f32[768,1536]{1,0:T(8,128)} fusion(bf16[16,196,768]{2,0,1:T(8,128)(2,1)} %all-gather.15.cloned.1.call-done, bf16[16,196,1536]{2,1,0:T(8,128)(2,1)} %get-tuple-element.242), kind=kOutput, calls=%fused_computation.79 | convolution fusion | flops 7398752256 | bytes 19169280 | tf_op jit(solution)/shard_map/gsd,gsf->df/dot_general | solution.py:127
  538.9 31.1 %reduce-scatter.16.cloned.1.call-done = bf16[8,196,768]{2,1,0:T(8,128)(2,1)} async-done(((bf16[16,196,768]{2,1,0:T(8,128)(2,1)}), bf16[8,196,768]{2,1,0:T(8,128)(2,1)}) %reduce-scatter.16.cloned.1.call-update) | async-done | bytes 2408464 | tf_op jit(solution)/shard_map/reduce_scatter | solution.py:129
  570.1 4.4 fusion.22
  574.5 4.2 fusion.26
  578.7 55.8 %reduce-scatter.14.cloned.1.call-done = bf16[8,196,768]{2,1,0:T(8,128)(2,1)} async-done(((bf16[16,196,768]{2,1,0:T(8,128)(2,1)}), bf16[8,196,768]{2,1,0:T(8,128)(2,1)}) %reduce-scatter.14.cloned.1.call-update) | async-done | bytes 2408464 | tf_op jit(solution)/shard_map/reduce_scatter | solution.py:116
  634.5 7.2 fusion.87
  641.7 2.2 copy-done.7
  643.9 3.7 convolution_convert_fusion.4
  647.6 3.1 copy.186
  650.7 18.1 %multiply_reduce_fusion = (f32[8,12,196]{2,1,0:T(8,128)S(1)}, f32[8,12,196,196]{2,3,1,0:T(8,128)}) fusion(f32[8,12,196,196]{2,3,1,0:T(8,128)} %get-tuple-element.229, f32[8,12,196]{2,1,0:T(8,128)S(1)} %copy-done.12, bf16[8,196,12,64]{1,3,2,0:T(8,128)(2,1)S(1)} %bitcast.115, f32[8,196,12,64]{1,3,2,0:T(8,128)} %bitcast.110, f32[12,64]{1,0:T(8,128)S(1)} %copy-done.43), kind=kOutput, calls=%fused_computation.9 | convolution fusion | flops 489197184 | bytes 36882432 | tf_op jit(solution)/shard_map/gqhe,gkhe->ghqk/dot_general | solution.py:144
  668.8 14.3 %multiply_convert_fusion = bf16[8,12,196,196]{2,3,1,0:T(8,128)(2,1)S(1)} fusion(f32[8,12,196,196]{2,3,1,0:T(8,128)} %get-tuple-element.234, f32[8,12,196,196]{2,3,1,0:T(8,128)} %get-tuple-element.229, f32[8,12,196]{2,1,0:T(8,128)S(1)} %get-tuple-element.233, f32[8,12,196]{2,1,0:T(8,128)S(1)} %copy-done.12), kind=kLoop, calls=%fused_computation.8 | loop fusion | flops 18439680 | bytes 37029888 | tf_op jit(solution)/shard_map/convert_element_type | solution.py:148
  683.2 4.2 bitcast_reduce_fusion.2
  687.8 4.7 copy.190
  692.5 10.7 %multiply_convert_fusion.2 = bf16[8,12,64,196]{3,2,1,0:T(8,128)(2,1)} fusion(bf16[8,12,196,196]{2,3,1,0:T(8,128)(2,1)} %copy-done.1, f32[8,196,12,64]{1,3,2,0:T(8,128)} %bitcast.112, f32[12,64]{1,0:T(8,128)S(1)} %copy-done.41), kind=kOutput, calls=%fused_computation.48 | convolution fusion | flops 476872704 | bytes 14604288 | tf_op jit(solution)/shard_map/ghqk,gqhe->gkhe/dot_general | solution.py:154
  703.3 4.5 copy.191
  707.8 6.8 bitcast_convert_fusion.1
  714.7 12.4 %bitcast_reduce_fusion.1 = (bf16[12,64]{1,0:T(8,128)(2,1)S(1)}, bf16[8,12,64,196]{3,2,1,0:T(8,128)(2,1)}) fusion(bf16[8,196,12,64]{1,3,2,0:T(8,128)(2,1)S(1)} %bitcast.116, f32[8,12,196,196]{2,3,1,0:T(8,128)} %get-tuple-element.229, f32[8,12,196]{2,1,0:T(8,128)S(1)} %copy-done.12), kind=kOutput, calls=%fused_computation.85 | convolution fusion | flops 485527296 | bytes 19645440 | tf_op jit(solution)/shard_map/ghqk,gqhe->gkhe/dot_general | solution.py:157
  727.1 5.1 copy.192
  732.3 13.1 %fusion.39 = bf16[3,768,768]{1,2,0:T(8,128)(2,1)} fusion(bf16[1,8,196,768]{3,2,0,1:T(8,128)(2,1)} %copy.192, bf16[1,8,196,768]{3,2,0,1:T(8,128)(2,1)} %copy.191, bf16[1,8,196,768]{3,2,0,1:T(8,128)(2,1)} %copy.190, f32[768]{0:T(1024)S(1)} %copy-done.59, f32[768]{0:T(1024)S(1)} %copy-done.47, f32[8,196]{1,0:T(8,128)S(1)} %copy-done.39, ...), kind=kOutput, calls=%fused_computation.81 | convolution fusion | flops 5565284352 | bytes 13191424 | tf_op jit(solution)/shard_map/gsd,cgsf->cdf/dot_general | solution.py:172
  748.6 2.0 multiply_add_fusion.2
  750.6 2.3 copy.219
  753.0 10.5 %fusion.24 = (f32[8,196]{1,0:T(8,128)S(1)}, f32[8,196,768,1]{2,1,3,0:T(8,128)S(1)}) fusion(f32[768]{0:T(1024)S(1)} %copy-done.47, f32[8,196]{1,0:T(8,128)S(1)} %copy-done.27, bf16[8,196,768]{2,0,1:T(8,128)(2,1)S(1)} %copy-done.3, bf16[3,768,768]{2,1,0:T(8,128)(2,1)} %all-gather.11.cloned.1.call-done, bf16[1,8,196,768]{3,2,0,1:T(8,128)(2,1)} %copy.192, ...), kind=kOutput, calls=%fused_computation.61 | convolution fusion | flops 5562309120 | bytes 18005248 | tf_op jit(solution)/shard_map/cgsf,cdf->gsd/dot_general | solution.py:175
  763.5 2.1 copy-done.8
  765.7 3.3 fusion.21
  769.0 24.8 %reduce-scatter.18.cloned.1.call-done = bf16[3,768,384]{1,2,0:T(8,128)(2,1)} async-done(((bf16[3,768,768]{1,2,0:T(8,128)(2,1)}), bf16[3,768,384]{1,2,0:T(8,128)(2,1)}) %reduce-scatter.18.cloned.1.call-update) | async-done | bytes 1769488 | tf_op jit(solution)/shard_map/reduce_scatter | solution.py:179
  793.8 5.6 copy.193
  799.4 5.0 add_add_fusion.2
  804.4 3.7 copy.204
  808.3 1.9 copy.203
  810.2 39.6 %all-reduce.4 = (f32[4,768]{1,0:T(4,128)S(1)}, f32[2,768]{1,0:T(2,128)S(1)}) all-reduce(f32[4,768]{1,0:T(4,128)S(1)} %pad_maximum_fusion.5, f32[2,768]{1,0:T(2,128)S(1)} %pad_maximum_fusion.6), channel_id=1, replica_groups=mesh['fsdp'=16,'tp'=2] {'fsdp','tp'}, use_global_device_ids=true, to_apply=%region_17.0 | all-reduce | flops 4608 | bytes 36864 | tf_op jit(solution)/shard_map/psum | solution.py:202
  852.0 61.8 %all-reduce.5 = (f32[2,384]{1,0:T(2,128)S(1)}, f32[1536]{0:T(1024)S(1)}) all-reduce(bf16[2,384]{1,0:T(2,128)(2,1)S(1)} %copy.216, f32[1536]{0:T(1024)S(1)} %copy-done.54), channel_id=7, replica_groups=mesh['fsdp'=16,'tp'=2] {'fsdp'}, use_global_device_ids=true, to_apply=%region_23.0.clone | all-reduce | flops 2304 | bytes 16896
  915.1 1.6 add_multiply_fusion
  916.7 72.7 %all-reduce.8.cloned.1.call-done = f32[3,768,384]{2,0,1:T(4,128)} async-done(((f32[3,768,384]{2,0,1:T(4,128)}), f32[3,768,384]{2,0,1:T(4,128)}) %all-reduce.8.cloned.1.call-update) | async-done | bytes 3538960
  (234 shorter events, 18.7 us)
Async XLA Ops:
  7.2 69.9 %copy-start.13 = (f32[48,1536]{1,0:T(8,128)S(1)}, f32[48,1536]{1,0:T(8,128)}, u32[]{:S(2)}) copy-start(f32[48,1536]{1,0:T(8,128)} %param.34) | copy-start | bytes 884740
  7.2 70.7 %copy-start.2 = (bf16[8,196,768]{2,0,1:T(8,128)(2,1)S(1)}, bf16[8,196,768]{2,0,1:T(8,128)(2,1)}, u32[]{:S(2)}) copy-start(bf16[8,196,768]{2,0,1:T(8,128)(2,1)} %param.27) | copy-start | bytes 7225348
  7.2 46.9 %all-gather.9.cloned.1.call-start = ((), (), s32[]{:S(2)}) async-start(), calls=%async_computation.8 | async-start | bytes 1880064 | tf_op jit(solution)/shard_map/all_gather | solution.py:74
  9.0 71.2 %copy-start.44 = (f32[4,768]{1,0:T(4,128)S(1)}, f32[4,768]{1,0:T(4,128)}, u32[]{:S(2)}) copy-start(f32[4,768]{1,0:T(4,128)} %param.30) | copy-start | bytes 36868
  9.1 71.2 %copy-start.63 = (f32[2,24]{1,0:T(2,128)S(1)}, f32[2,24]{1,0:T(2,128)}, u32[]{:S(2)}) copy-start(f32[2,24]{1,0:T(2,128)} %param.32) | copy-start | bytes 580
  9.1 94.9 %all-gather.11.cloned.1.call-start = ((), (), s32[]{:S(2)}) async-start(), calls=%async_computation.9 | async-start | bytes 5308416 | tf_op jit(solution)/shard_map/all_gather | solution.py:85
  54.1 48.2 %copy-start.48 = (f32[2,768]{1,0:T(2,128)S(1)}, f32[2,768]{1,0:T(2,128)}, u32[]{:S(2)}) copy-start(f32[2,768]{1,0:T(2,128)} %param.37) | copy-start | bytes 18436
  54.1 131.7 %all-gather.13.cloned.1.call-start = ((), (), s32[]{:S(2)}) async-start(), calls=%async_computation.10 | async-start | bytes 1769472 | tf_op jit(solution)/shard_map/all_gather | solution.py:87
  77.1 156.8 %all-gather.17.cloned.1.call-start = ((), (), s32[]{:S(2)}) async-start(), calls=%async_computation.12 | async-start | bytes 2506752 | tf_op jit(solution)/shard_map/all_gather | solution.py:79
  77.8 182.0 %all-gather.15.cloned.1.call-start = ((), (), s32[]{:S(2)}) async-start(), calls=%async_computation.11 | async-start | bytes 7225344 | tf_op jit(solution)/shard_map/all_gather | solution.py:109
  78.6 37.3 %copy-start.26 = (f32[8,196]{1,0:T(8,128)}, f32[8,196]{1,0:T(8,128)S(1)}, u32[]{:S(2)}) copy-start(f32[8,196]{1,0:T(8,128)S(1)} %broadcast_multiply_fusion.1) | copy-start | bytes 18820
  80.2 35.7 %copy-start.38 = (f32[8,196]{1,0:T(8,128)}, f32[8,196]{1,0:T(8,128)S(1)}, u32[]{:S(2)}) copy-start(f32[8,196]{1,0:T(8,128)S(1)} %fusion.68) | copy-start | bytes 18820
  80.3 35.6 %copy-start.46 = (f32[768]{0:T(1024)}, f32[768]{0:T(1024)S(1)}, u32[]{:S(2)}) copy-start(f32[768]{0:T(1024)S(1)} %get-tuple-element.180) | copy-start | bytes 9220
  80.3 35.6 %copy-start.58 = (f32[768]{0:T(1024)}, f32[768]{0:T(1024)S(1)}, u32[]{:S(2)}) copy-start(f32[768]{0:T(1024)S(1)} %get-tuple-element.179) | copy-start | bytes 9220
  80.3 112.5 %copy-start.30 = (f32[768]{0:T(1024)}, f32[768]{0:T(1024)S(1)}, u32[]{:S(2)}) copy-start(f32[768]{0:T(1024)S(1)} %get-tuple-element.178) | copy-start | bytes 9220
  102.2 37.0 %copy-start.40 = (f32[12,64]{1,0:T(8,128)}, f32[12,64]{1,0:T(8,128)S(1)}, u32[]{:S(2)}) copy-start(f32[12,64]{1,0:T(8,128)S(1)} %reshape.215) | copy-start | bytes 9220
  102.3 69.4 %copy-start.42 = (f32[12,64]{1,0:T(8,128)}, f32[12,64]{1,0:T(8,128)S(1)}, u32[]{:S(2)}) copy-start(f32[12,64]{1,0:T(8,128)S(1)} %reshape.214) | copy-start | bytes 9220
  171.7 14.2 %copy-start.11 = (f32[8,12,196]{2,1,0:T(8,128)}, f32[8,12,196]{2,1,0:T(8,128)S(1)}, u32[]{:S(2)}) copy-start(f32[8,12,196]{2,1,0:T(8,128)S(1)} %log_add_fusion) | copy-start | bytes 225796
  195.7 133.2 %all-gather.21.cloned.1.call-start = ((), (), s32[]{:S(2)}) async-start(), calls=%async_computation.15 | async-start | bytes 7225344 | tf_op jit(solution)/shard_map/all_gather | solution.py:121
  199.1 222.4 %reduce-scatter.24.cloned.1.call-start = ((), (), s32[]{:S(2)}) async-start(), calls=%async_computation.20 | async-start | bytes 5013504 | tf_op jit(solution)/shard_map/reduce_scatter | solution.py:198
  345.8 75.7 %copy-start.16 = (f32[1536,48]{0,1:T(8,128)S(1)}, f32[1536,48]{0,1:T(8,128)}, u32[]{:S(2)}) copy-start(f32[1536,48]{0,1:T(8,128)} %param.36) | copy-start | bytes 884740
  345.8 75.7 %copy-start.17 = (f32[1536,48]{0,1:T(8,128)S(1)}, f32[1536,48]{0,1:T(8,128)}, u32[]{:S(2)}) copy-start(f32[1536,48]{0,1:T(8,128)} %param.44) | copy-start | bytes 884740
  345.8 75.7 %copy-start.18 = (f32[1536,48]{0,1:T(8,128)S(1)}, f32[1536,48]{0,1:T(8,128)}, u32[]{:S(2)}) copy-start(f32[1536,48]{0,1:T(8,128)} %param.52) | copy-start | bytes 884740
  345.8 120.1 %all-gather.19.cloned.1.call-start = ((), (), s32[]{:S(2)}) async-start(), calls=%async_computation.13 | async-start | bytes 2506752 | tf_op jit(solution)/shard_map/all_gather | solution.py:81
  423.6 146.5 %reduce-scatter.16.cloned.1.call-start = ((), (), s32[]{:S(2)}) async-start(), calls=%async_computation.16 | async-start | bytes 7372800 | tf_op jit(solution)/shard_map/reduce_scatter | solution.py:129
  465.9 29.5 %copy-start.71 = (bf16[768,1536]{1,0:T(8,128)(2,1)S(1)}, bf16[768,1536]{1,0:T(8,128)(2,1)}, u32[]{:S(2)}) copy-start(bf16[768,1536]{1,0:T(8,128)(2,1)} %all-gather.17.cloned.1.call-done) | copy-start | bytes 7077892
  509.0 125.5 %reduce-scatter.14.cloned.1.call-start = ((), (), s32[]{:S(2)}) async-start(), calls=%async_computation.14 | async-start | bytes 7372800 | tf_op jit(solution)/shard_map/reduce_scatter | solution.py:116
  524.7 45.4 %copy-start.23 = (f32[8,196]{1,0:T(8,128)S(1)}, f32[8,196]{1,0:T(8,128)}, u32[]{:S(2)}) copy-start(f32[8,196]{1,0:T(8,128)} %copy-done.22) | copy-start | bytes 18820
  524.7 45.4 %copy-start.31 = (f32[768]{0:T(1024)S(1)}, f32[768]{0:T(1024)}, u32[]{:S(2)}) copy-start(f32[768]{0:T(1024)} %copy-done.30) | copy-start | bytes 9220
  524.7 223.8 %reduce-scatter.22.cloned.1.call-start = ((), (), s32[]{:S(2)}) async-start(), calls=%async_computation.19 | async-start | bytes 5013504 | tf_op jit(solution)/shard_map/reduce_scatter | solution.py:196
  538.9 35.6 %copy-start.35 = (f32[8,196]{1,0:T(8,128)S(1)}, f32[8,196]{1,0:T(8,128)}, u32[]{:S(2)}) copy-start(f32[8,196]{1,0:T(8,128)} %copy-done.34) | copy-start | bytes 18820
  538.9 35.6 %copy-start.29 = (f32[8,196]{1,0:T(8,128)S(1)}, f32[8,196]{1,0:T(8,128)}, u32[]{:S(2)}) copy-start(f32[8,196]{1,0:T(8,128)} %copy-done.28) | copy-start | bytes 18820
  538.9 211.7 %reduce-scatter.20.cloned.1.call-start = ((), (), s32[]{:S(2)}) async-start(), calls=%async_computation.18 | async-start | bytes 1769472 | tf_op jit(solution)/shard_map/reduce_scatter | solution.py:185
  574.4 60.0 %copy-start.50 = (f32[768]{0:T(1024)S(1)}, f32[768]{0:T(1024)}, u32[]{:S(2)}) copy-start(f32[768]{0:T(1024)} %get-tuple-element.182) | copy-start | bytes 9220
  574.5 60.0 %copy-start.61 = (f32[8]{0:T(128)S(1)}, f32[8]{0:T(128)}, u32[]{:S(2)}) copy-start(f32[8]{0:T(128)} %copy-done.60) | copy-start | bytes 100
  668.8 14.3 %copy-start.4 = (bf16[1,8,196,768]{2,3,1,0:T(8,128)(2,1)S(1)}, bf16[1,8,196,768]{2,3,1,0:T(8,128)(2,1)}, u32[]{:S(2)}) copy-start(bf16[1,8,196,768]{2,3,1,0:T(8,128)(2,1)} %copy.177) | copy-start | bytes 7225348
  714.7 79.1 %reduce-scatter.18.cloned.1.call-start = ((), (), s32[]{:S(2)}) async-start(), calls=%async_computation.17 | async-start | bytes 5308416 | tf_op jit(solution)/shard_map/reduce_scatter | solution.py:179
  732.3 16.3 %copy-start.14 = (f32[48,1536]{1,0:T(8,128)S(1)}, f32[48,1536]{1,0:T(8,128)}, u32[]{:S(2)}) copy-start(f32[48,1536]{1,0:T(8,128)} %param.34) | copy-start | bytes 884740
  732.3 16.3 %copy-start.20 = (f32[48,1536]{1,0:T(8,128)S(1)}, f32[48,1536]{1,0:T(8,128)}, u32[]{:S(2)}) copy-start(f32[48,1536]{1,0:T(8,128)} %param.42) | copy-start | bytes 884740
  732.3 16.3 %copy-start.21 = (f32[48,1536]{1,0:T(8,128)S(1)}, f32[48,1536]{1,0:T(8,128)}, u32[]{:S(2)}) copy-start(f32[48,1536]{1,0:T(8,128)} %param.50) | copy-start | bytes 884740
  745.4 105.6 %reduce-scatter.26.cloned.1.call-start = ((), (), s32[]{:S(2)}) async-start(), calls=%async_computation.21 | async-start | bytes 294912
  748.5 166.6 %reduce-scatter.28.cloned.1.call-start = ((), (), s32[]{:S(2)}) async-start(), calls=%async_computation.22 | async-start | bytes 1253376
  753.0 236.5 %all-reduce.8.cloned.1.call-start = ((), (), s32[]{:S(2)}) async-start(), calls=%async_computation.23 | async-start | bytes 9437184
  804.4 45.4 %copy-start.49 = (f32[2,768]{1,0:T(2,128)S(1)}, f32[2,768]{1,0:T(2,128)}, u32[]{:S(2)}) copy-start(f32[2,768]{1,0:T(2,128)} %param.37) | copy-start | bytes 18436
  804.4 45.4 %copy-start.55 = (f32[2,768]{1,0:T(2,128)S(1)}, f32[2,768]{1,0:T(2,128)}, u32[]{:S(2)}) copy-start(f32[2,768]{1,0:T(2,128)} %param.45) | copy-start | bytes 18436
  804.4 45.4 %copy-start.56 = (f32[2,768]{1,0:T(2,128)S(1)}, f32[2,768]{1,0:T(2,128)}, u32[]{:S(2)}) copy-start(f32[2,768]{1,0:T(2,128)} %param.53) | copy-start | bytes 18436
  808.1 42.3 %copy-start.45 = (f32[4,768]{1,0:T(4,128)S(1)}, f32[4,768]{1,0:T(4,128)}, u32[]{:S(2)}) copy-start(f32[4,768]{1,0:T(4,128)} %param.30) | copy-start | bytes 36868
  808.1 42.3 %copy-start.51 = (f32[4,768]{1,0:T(4,128)S(1)}, f32[4,768]{1,0:T(4,128)}, u32[]{:S(2)}) copy-start(f32[4,768]{1,0:T(4,128)} %param.38) | copy-start | bytes 36868
  808.1 42.3 %copy-start.52 = (f32[4,768]{1,0:T(4,128)S(1)}, f32[4,768]{1,0:T(4,128)}, u32[]{:S(2)}) copy-start(f32[4,768]{1,0:T(4,128)} %param.46) | copy-start | bytes 36868
  808.1 43.9 %copy-start.54 = (f32[1536]{0:T(1024)S(1)}, f32[1536]{0:T(1024)}, u32[]{:S(2)}) copy-start(f32[1536]{0:T(1024)} %get-tuple-element.241) | copy-start | bytes 18436
  808.1 105.7 %copy-start.68 = (f32[96]{0:T(128)S(1)}, f32[96]{0:T(128)}, u32[]{:S(2)}) copy-start(f32[96]{0:T(128)} %param.35) | copy-start | bytes 1156
  808.1 105.7 %copy-start.69 = (f32[96]{0:T(128)S(1)}, f32[96]{0:T(128)}, u32[]{:S(2)}) copy-start(f32[96]{0:T(128)} %param.43) | copy-start | bytes 1156
  808.1 105.7 %copy-start.70 = (f32[96]{0:T(128)S(1)}, f32[96]{0:T(128)}, u32[]{:S(2)}) copy-start(f32[96]{0:T(128)} %param.51) | copy-start | bytes 1156
  808.1 106.3 %copy-start.64 = (f32[2,24]{1,0:T(2,128)S(1)}, f32[2,24]{1,0:T(2,128)}, u32[]{:S(2)}) copy-start(f32[2,24]{1,0:T(2,128)} %param.32) | copy-start | bytes 580
  808.1 106.3 %copy-start.65 = (f32[2,24]{1,0:T(2,128)S(1)}, f32[2,24]{1,0:T(2,128)}, u32[]{:S(2)}) copy-start(f32[2,24]{1,0:T(2,128)} %param.40) | copy-start | bytes 580
  808.2 106.3 %copy-start.66 = (f32[2,24]{1,0:T(2,128)S(1)}, f32[2,24]{1,0:T(2,128)}, u32[]{:S(2)}) copy-start(f32[2,24]{1,0:T(2,128)} %param.48) | copy-start | bytes 580
  808.2 106.9 %copy-start.19 = (f32[384,48]{0,1:T(8,128)S(1)}, f32[384,48]{0,1:T(8,128)}, u32[]{:S(2)}) copy-start(f32[384,48]{0,1:T(8,128)} %param.33) | copy-start | bytes 221188
  808.2 106.9 %copy-start.36 = (f32[384,48]{0,1:T(8,128)S(1)}, f32[384,48]{0,1:T(8,128)}, u32[]{:S(2)}) copy-start(f32[384,48]{0,1:T(8,128)} %param.41) | copy-start | bytes 221188
  808.2 106.9 %copy-start.37 = (f32[384,48]{0,1:T(8,128)S(1)}, f32[384,48]{0,1:T(8,128)}, u32[]{:S(2)}) copy-start(f32[384,48]{0,1:T(8,128)} %param.49) | copy-start | bytes 221188
  808.2 182.3 %copy-start.15 = (f32[3,48,384]{2,1,0:T(8,128)S(1)}, f32[3,48,384]{2,1,0:T(8,128)}, u32[]{:S(2)}) copy-start(f32[3,48,384]{2,1,0:T(8,128)} %param.31) | copy-start | bytes 663556
  808.2 182.3 %copy-start.24 = (f32[3,48,384]{2,1,0:T(8,128)S(1)}, f32[3,48,384]{2,1,0:T(8,128)}, u32[]{:S(2)}) copy-start(f32[3,48,384]{2,1,0:T(8,128)} %param.39) | copy-start | bytes 663556
  808.2 182.3 %copy-start.25 = (f32[3,48,384]{2,1,0:T(8,128)S(1)}, f32[3,48,384]{2,1,0:T(8,128)}, u32[]{:S(2)}) copy-start(f32[3,48,384]{2,1,0:T(8,128)} %param.47) | copy-start | bytes 663556
  849.8 141.7 %copy-start.53 = (f32[4,768]{1,0:T(4,128)}, f32[4,768]{1,0:T(4,128)S(1)}, u32[]{:S(2)}) copy-start(f32[4,768]{1,0:T(4,128)S(1)} %get-tuple-element.186) | copy-start | bytes 36868
  849.8 141.7 %copy-start.57 = (f32[2,768]{1,0:T(2,128)}, f32[2,768]{1,0:T(2,128)S(1)}, u32[]{:S(2)}) copy-start(f32[2,768]{1,0:T(2,128)S(1)} %get-tuple-element.187) | copy-start | bytes 18436
  (26 other events, 100.0 us)
Sparse Core Ops, SparseCore 0:
  11.0 43.1 all-gather.8
  55.7 48.2 all-gather.10
  106.1 22.7 all-gather.12
  131.6 42.2 all-gather.16
  195.9 63.9 all-gather.14
  261.8 63.7 all-gather.20
  345.9 75.5 reduce-scatter.23
  424.6 41.2 all-gather.18
  509.1 60.8 reduce-scatter.15
  572.3 62.0 reduce-scatter.13
  639.4 75.5 reduce-scatter.21
  717.7 20.8 reduce-scatter.19
  745.5 48.2 reduce-scatter.17
  796.5 10.9 reduce-scatter.25
  811.5 58.1 reduce-scatter.27
  873.1 116.2 all-reduce.7
where the time goes:
time: 1010 us; the launch traced here: 998 us
  waiting for transfers between devices  375 us (37%)
  matrix products  230 us (23%)
  blocking collectives  177 us (18%)
  other arithmetic  112 us (11%)
  local copies, waits for them, and re-layouts  85.6 us (8%)
  between operations  18.4 us (2%)
    unnamed x2, blocking collectives  94.8 us
    reduce_scatter x1, waiting for transfers between devices, per_device(): lax.psum_scatter(grad_w2, 'fsdp', scatter_dimension=1, tiled=True)  75.6 us
    unnamed x19, waiting for transfers between devices  73 us
    reduce_scatter x1, waiting for transfers between devices, per_device(): lax.psum_scatter(mlp_part.astype(jnp.bfloat16), 'tp', scatter_dimension=0...  55.8 us
    convert_element_type x1, other arithmetic, per_device(): activated = exact_gelu(pre_act).astype(jnp.bfloat16)  45.1 us
    all_gather x1, waiting for transfers between devices, per_device(): lax.all_gather(w_qkv.astype(jnp.bfloat16), 'fsdp', axis=1, tiled=True)  45 us
    all_gather x1, waiting for transfers between devices, per_device(): lax.all_gather(w_fc2.astype(jnp.bfloat16), 'fsdp', axis=1, tiled=True)  42.2 us
    psum x1, blocking collectives, per_device(): g_norm, g_bout = lax.psum((norm_terms, bias_terms), ('fsdp', 'tp'))  39.6 us
  transfers between devices with their start and end apart: 16, of which 9 were waited for; matrix products, arithmetic and copies ran while one was open for 35% of the time, Pallas kernels for 0%

commit v1 on v0

--- a/solution.py
+++ b/solution.py
@@ -1,6 +1,10 @@
+import functools
+
 import jax
 import jax.numpy as jnp
 from jax import lax
+from jax.experimental import pallas as pl
+from jax.experimental.pallas import tpu as pltpu
 from jax.sharding import PartitionSpec as P
 
 HEAD_DIM = 64
@@ -246,6 +250,1048 @@
     )
 
 
+F32, BF16 = jnp.float32, jnp.bfloat16
+MESH_IDS = pl.DeviceIdType.MESH
+VMEM_BYTES = 62 * 2**20
+
+NZ, NY, NCORE, NTP = 4, 2, 2, 2
+HALF = 256
+NEG = -1e30
+LANES = 256
+
+
+def dot(a, b, ca, cb):
+    return lax.dot_general(a, b, (((ca,), (cb,)), ((), ())), preferred_element_type=F32)
+
+
+def normed(v):
+    centre = v - jnp.mean(v, axis=-1, keepdims=True)
+    rstd = lax.rsqrt(jnp.mean(centre * centre, axis=-1, keepdims=True) + norm_eps)
+    return centre * rstd, rstd
+
+
+def norm_back(e, gain, xhat, rstd):
+    eg = e * gain
+    m1 = jnp.mean(eg, axis=-1, keepdims=True)
+    m2 = jnp.mean(eg * xhat, axis=-1, keepdims=True)
+    return rstd * (eg - m1 - xhat * m2)
+
+
+def pad_rows(v, rows):
+    return jnp.concatenate([v, jnp.zeros((rows - v.shape[0], v.shape[1]), v.dtype)], axis=0)
+
+
+def load_columns(ref, r):
+    return jnp.concatenate([ref[j, r, :] for j in range(ref.shape[0])], axis=1)
+
+
+def store_columns(ref, r, v):
+    for j in range(ref.shape[0]):
+        ref[j, r, :] = v[:, 128 * j : 128 * j + 128]
+
+
+class Place:
+    def __init__(self):
+        f = lax.axis_index("fsdp")
+        self.x = lax.axis_index("tp")
+        self.z = f // (NY * NCORE)
+        self.y = lax.rem(f // NCORE, NY)
+        self.c = lax.rem(f, NCORE)
+        self.sib = self.at(self.z, self.y, 1 - self.c, self.x)
+        self.peer_x = self.at(self.z, self.y, self.c, 1 - self.x)
+        self.peer_y = self.at(self.z, 1 - self.y, self.c, self.x)
+        self.other_z = [lax.rem(self.z + d, NZ) for d in range(1, NZ)]
+        self.peers_z = [self.at(o, self.y, self.c, self.x) for o in self.other_z]
+        self.lanes = pl.ds(pl.multiple_of(self.x * HALF, HALF), HALF)
+        self.lanes_other = pl.ds(pl.multiple_of((1 - self.x) * HALF, HALF), HALF)
+
+    def pick(self, v):
+        return jnp.where(self.x == 0, v[..., :HALF], v[..., HALF:])
+
+    def at(self, z, y, c, x):
+        return {"fsdp": (z * NY + y) * NCORE + c, "tp": x}
+
+    def barrier(self):
+        sem = pltpu.get_barrier_semaphore()
+        everyone = [self.sib, self.peer_x, self.peer_y] + self.peers_z
+        for d in everyone:
+            pl.semaphore_signal(sem, inc=1, device_id=d, device_id_type=MESH_IDS)
+        pl.semaphore_wait(sem, len(everyone))
+
+
+def remote(src, dst, send, recv, device):
+    return pltpu.make_async_remote_copy(
+        src_ref=src, dst_ref=dst, send_sem=send, recv_sem=recv, device_id=device, device_id_type=MESH_IDS
+    )
+
+
+def start_all(copies):
+    for k in copies:
+        k.start()
+
+
+def wait_all(copies):
+    for k in copies:
+        k.wait()
+
+
+AG_SEMS = 7
+
+
+def gather_steps(at, buf, own, send, recv, local, y_first):
+    x, y, z, c, lanes = at.x, at.y, at.z, at.c, at.lanes
+    mine = buf.at[z, y, c, :, lanes]
+    keep = pltpu.make_async_copy(own, mine, local)
+    s0 = [remote(own, mine, send.at[d], recv.at[d], at.peers_z[d]) for d in range(NZ - 1)]
+    line = buf.at[:, y, c, :, lanes]
+    s1 = remote(line, line, send.at[3], recv.at[3], at.peer_y if y_first else at.peer_x)
+    if y_first:
+        plane, rest = buf.at[:, :, c, :, lanes], buf.at[:, :, c, :, at.lanes_other]
+    else:
+        plane, rest = buf.at[:, y, c], buf.at[:, 1 - y, c]
+    s2 = remote(plane, plane, send.at[4], recv.at[4], at.peer_x if y_first else at.peer_y)
+    sib_a = remote(plane, plane, send.at[5], recv.at[5], at.sib)
+    sib_b = remote(rest, rest, send.at[6], recv.at[6], at.sib)
+
+    def step0():
+        keep.start()
+        start_all(s0)
+
+    def step1():
+        keep.wait()
+        wait_all(s0)
+        s1.start()
+
+    def step2():
+        s1.wait()
+        s2.start()
+        sib_a.start()
+
+    def step3():
+        s2.wait()
+        sib_b.start()
+
+    def step4():
+        sib_a.wait()
+        sib_b.wait()
+
+    return [step0, step1, step2, step3, step4]
+
+
+RS_SEMS = 6
+
+
+def scatter_steps(at, grad, r0, r1, r2, r3, out, send, recv, x_first):
+    x, y, z, c = at.x, at.y, at.z, at.c
+    s0 = remote(grad.at[:, :, 1 - c], r0, send.at[0], recv.at[0], at.sib)
+    if x_first:
+        s1 = remote(r0.at[:, :, :, at.lanes_other], r1, send.at[1], recv.at[1], at.peer_x)
+        s2 = remote(r1.at[:, 1 - y], r2, send.at[2], recv.at[2], at.peer_y)
+    else:
+        s1 = remote(r0.at[:, 1 - y], r1, send.at[1], recv.at[1], at.peer_y)
+        s2 = remote(r1.at[:, :, at.lanes_other], r2, send.at[2], recv.at[2], at.peer_x)
+    s3 = [
+        remote(r2.at[at.other_z[d]], r3.at[d], send.at[3 + d], recv.at[3 + d], at.peers_z[d])
+        for d in range(NZ - 1)
+    ]
+
+    def add(a, b):
+        return (a.astype(F32) + b.astype(F32)).astype(BF16)
+
+    def step0():
+        s0.start()
+
+    def step1():
+        s0.wait()
+
+        def body(k, _):
+            r0[k] = add(r0[k], grad[k, :, c])
+            return 0
+
+        lax.fori_loop(0, NZ, body, 0)
+        s1.start()
+
+    def step2():
+        s1.wait()
+
+        def body(k, _):
+            r1[k] = add(r1[k], at.pick(r0[k]) if x_first else r0[k, y])
+            return 0
+
+        lax.fori_loop(0, NZ, body, 0)
+        s2.start()
+
+    def step3():
+        s2.wait()
+
+        def body(k, _):
+            r2[k] = add(r2[k], r1[k, y] if x_first else at.pick(r1[k]))
+            return 0
+
+        lax.fori_loop(0, NZ, body, 0)
+        start_all(s3)
+
+    def step4():
+        wait_all(s3)
+        total = r2[z].astype(F32)
+        for d in range(NZ - 1):
+            total = total + r3[d].astype(F32)
+        out[...] = total
+
+    return [step0, step1, step2, step3, step4]
+
+
+def scatter_scratch(chunks, rows):
+    wide = NTP * HALF
+    return [
+        pltpu.VMEM((chunks, 2, NZ, NY, rows, wide), BF16),
+        pltpu.VMEM((chunks, NZ, NY, rows, HALF), BF16),
+        pltpu.VMEM((chunks, NZ, rows, wide), BF16),
+        pltpu.VMEM((chunks, 2, NZ, rows, HALF), BF16),
+        pltpu.VMEM((chunks, 2, NZ - 1, rows, HALF), BF16),
+        pltpu.SemaphoreType.DMA((chunks, 2, RS_SEMS)),
+        pltpu.SemaphoreType.DMA((chunks, 2, RS_SEMS)),
+    ]
+
+
+def scatter_both(at, k, grads, scratch, outs):
+    r0, r1a, r1b, r2, r3, send, recv = scratch
+    first = scatter_steps(
+        at, grads[0], r0.at[k, 0], r1a.at[k], r2.at[k, 0], r3.at[k, 0], outs[0], send.at[k, 0], recv.at[k, 0], True
+    )
+    second = scatter_steps(
+        at, grads[1], r0.at[k, 1], r1b.at[k], r2.at[k, 1], r3.at[k, 1], outs[1], send.at[k, 1], recv.at[k, 1], False
+    )
+    return [both(a, b) for a, b in zip(first, second)]
+
+
+def both(a, b):
+    def run():
+        a()
+        b()
+
+    return run
+
+
+def gather_both(at, buf, own, sems):
+    send, recv, local = sems
+    first = gather_steps(at, buf.at[0], own.at[0], send.at[0], recv.at[0], local.at[0], True)
+    second = gather_steps(at, buf.at[1], own.at[1], send.at[1], recv.at[1], local.at[1], False)
+    return [both(a, b) for a, b in zip(first, second)]
+
+
+def run_slot(plan, key, counters):
+    for want, steps in plan.get(key, {}).items():
+        cond = None
+        for have, value in zip(counters, want):
+            test = have == value
+            cond = test if cond is None else jnp.logical_and(cond, test)
+
+        def go(steps=steps):
+            for s in steps:
+                s()
+
+        pl.when(cond)(go)
+
+
+def planned(entries):
+    plan = {}
+    for key, want, step in entries:
+        plan.setdefault(key, {}).setdefault(want, []).append(step)
+    return plan
+
+
+def matrix(ref):
+    v = ref[...]
+    return v.reshape(v.shape[0] * v.shape[1] * v.shape[2] * v.shape[3], v.shape[4])
+
+
+def left_half(rows):
+    return lax.broadcasted_iota(jnp.int32, (rows, 2 * HEAD_DIM), 1) < HEAD_DIM
+
+
+def split_heads(v, left):
+    zero = jnp.zeros_like(v)
+    return jnp.concatenate([jnp.where(left, v, zero), jnp.where(left, zero, v)], axis=0)
+
+
+def projection(a, b):
+    return jnp.concatenate([a, b[:, 0:128], b[:, HALF : HALF + 128]], axis=1)
+
+
+def out_columns(b):
+    return jnp.concatenate([b[:, 128:HALF], b[:, HALF + 128 :]], axis=1)
+
+
+def spread(pieces, width, row, total):
+    col = lax.broadcasted_iota(jnp.int32, (128, total), 1).astype(F32)
+    lane = lax.broadcasted_iota(jnp.int32, (128, total), 0).astype(F32)
+    owner = jnp.floor((col + 0.5) * (1.0 / width))
+    pick = (col - owner * width == lane).astype(BF16)
+    spreaded = dot(pieces.astype(BF16), pick, 1, 0)
+    at_row = lax.broadcasted_iota(jnp.int32, spreaded.shape, 0).astype(F32)
+    col = lax.broadcasted_iota(jnp.int32, spreaded.shape, 1).astype(F32)
+    owner = jnp.floor((col + 0.5) * (1.0 / width))
+    return jnp.sum(jnp.where(at_row == owner * 8.0 + row, spreaded, 0.0), axis=0, keepdims=True)
+
+
+def attention_kernel(
+    dims,
+    x_hbm, norm_ref, bout_ref, wqkv_ref, wout_ref, wfc1_ref, wfc2_ref, bqv_ref, bfc1_ref,
+    qkv_hbm, ctx_hbm, mid_hbm, p_hbm, watt_hbm, wff_hbm, own_hbm, bias_ref,
+    x_s, h1, qkv_s, ctx_s, mid_s, p_s, watt, own, pieces, bias_s,
+    ag_send, ag_recv, ag_local, sm_send, sm_recv, out_sem, in_sem,
+):
+    images, seq, sp, groups, chunks, early = dims
+    at = Place()
+    x_copy = pltpu.make_async_copy(x_hbm, x_s, in_sem.at[0])
+    x_copy.start()
+    own_rows = wqkv_ref.shape[2]
+    rows = images * seq
+    for g in range(groups):
+        cols = slice(128 * g, 128 * g + 128)
+        own[g, 0] = jnp.concatenate([wqkv_ref[0, :, cols], wqkv_ref[1, :, cols]], axis=1).astype(BF16)
+        own[g, 1] = jnp.concatenate([wqkv_ref[2, :, cols], wout_ref[:, cols]], axis=1).astype(BF16)
+    pieces[at.x, at.z, at.y, at.c] = jnp.zeros((8, 128), F32)
+    pieces[at.x, at.z, at.y, at.c, 0:1, 0 : bfc1_ref.shape[1]] = bfc1_ref[...]
+    pieces[at.x, at.z, at.y, at.c, 1:3, 0 : bqv_ref.shape[1]] = bqv_ref[...]
+
+    def sems(k):
+        return ag_send.at[k], ag_recv.at[k], ag_local.at[k]
+
+    steps = [gather_both(at, watt.at[g], own.at[g], sems(g)) for g in range(groups)]
+    steps += [gather_both(at, wff_hbm.at[f], own.at[groups + f], sems(groups + f)) for f in range(early)]
+    here = pieces.at[at.x, at.z, at.y, at.c]
+    line = pieces.at[at.x, :, at.y, at.c]
+    plane = pieces.at[at.x, :, :, at.c]
+    cube = pieces.at[:, :, :, at.c]
+    bias_steps = [[remote(here, here, sm_send.at[d], sm_recv.at[d], at.peers_z[d]) for d in range(NZ - 1)]]
+    bias_steps += [
+        [remote(r, r, sm_send.at[3 + k], sm_recv.at[3 + k], d)]
+        for k, (r, d) in enumerate([(line, at.peer_y), (plane, at.peer_x), (cube, at.sib)])
+    ]
+
+    at.barrier()
+    steps[0][0]()
+    start_all(bias_steps[0])
+    steps[1][0]()
+    for f in range(chunks - groups):
+        cols = slice(HALF * f, HALF * f + HALF)
+        own[groups + f, 0] = wfc1_ref[:, cols].astype(BF16)
+        own[groups + f, 1] = wfc2_ref[:, cols].astype(BF16)
+    late = pltpu.make_async_copy(own.at[pl.ds(groups + early, chunks - groups - early)], own_hbm, in_sem.at[1])
+    late.start()
+    x_copy.wait()
+
+    block = rows // 7
+
+    def first_norm(j, _):
+        r = pl.ds(pl.multiple_of(j * block, 16), block)
+        xhat, _r = normed(x_s[r, :].astype(F32))
+        store_columns(mid_s, r, xhat * norm_ref[0:1, :] + norm_ref[1:2, :])
+        return 0
+
+    def by_image(i, _):
+        h = pad_rows(load_columns(mid_s, pl.ds(i, seq, stride=images)), sp)
+        h1[pl.ds(pl.multiple_of(i * sp, 16), sp), :] = h.astype(BF16)
+        return 0
+
+    lax.fori_loop(0, 7, first_norm, 0)
+    steps[0][1]()
+    wait_all(bias_steps[0])
+    start_all(bias_steps[1])
+    steps[2][0]()
+    lax.fori_loop(0, images, by_image, 0)
+    steps[0][2]()
+    wait_all(bias_steps[1])
+    start_all(bias_steps[2])
+    steps[1][1]()
+    steps[0][3]()
+    wait_all(bias_steps[2])
+    start_all(bias_steps[3])
+    steps[1][2]()
+    wait_all(bias_steps[3])
+    flat = pieces[...].reshape(NTP * NZ * NY * NCORE * 8, 128)
+    width = bqv_ref.shape[1]
+    model = width * NTP * NZ * NY * NCORE
+    bias_q = spread(flat, width, 1.0, model)
+    bias_v = spread(flat, width, 2.0, model)
+    for g in range(groups):
+        parts = []
+        for t in range(NTP):
+            parts += [bias_q[:, t * own_rows + 128 * g : t * own_rows + 128 * g + 128], jnp.zeros((1, 128), F32)]
+        for t in range(NTP):
+            parts.append(bias_v[:, t * own_rows + 128 * g : t * own_rows + 128 * g + 128])
+        bias_s[g] = jnp.concatenate(parts, axis=1)
+    width = bfc1_ref.shape[1]
+    bias_ff = spread(flat, width, 0.0, width * NTP * NZ * NY * NCORE)
+    per = bias_ff.shape[1] // NTP
+    for f in range(chunks - groups):
+        bias_ref[f] = jnp.concatenate(
+            [bias_ff[:, t * per + f * HALF : t * per + f * HALF + HALF] for t in range(NTP)], axis=1
+        )
+    steps[0][4]()
+
+    when = {1: [None, None, None, (0, 1), (1, 0)], 2: [None, (0, 1), (0, 3), (1, 1), (2, 0)]}
+    place = [[(0, 3), (1, 1), (1, 3), (2, 1), (2, 3)], [(1, 2), (2, 0), (2, 2), (3, 0), (3, 2)]]
+    for f in range(early):
+        when[groups + f] = place[f]
+    plan = planned(
+        [("out" if w[0] == groups else "tile", w[1:] if w[0] == groups else w, steps[k][s])
+         for k, ws in when.items() for s, w in enumerate(ws) if w is not None]
+    )
+
+    pair = 2
+    tr = pair * sp
+    left = left_half(sp)
+    live_key = lax.broadcasted_iota(jnp.int32, (sp, sp), 0) < seq
+    tiles = images // pair
+
+    def group(g, _):
+        def tile(i, _):
+            run_slot(plan, "tile", (g, i))
+            r = pl.ds(pl.multiple_of(i * tr, 16), tr)
+            w = projection(matrix(watt.at[g, 0]), matrix(watt.at[g, 1]))
+            qkv = (dot(h1[r, :], w, 1, 0) + bias_s[g]).astype(BF16)
+            qkv_s[g, r, :] = qkv
+            for a in range(pair):
+                part = qkv[a * sp : (a + 1) * sp]
+                for t in range(NTP):
+                    q = part[:, t * HALF : t * HALF + 128] * jnp.asarray(HEAD_DIM ** (-0.5), BF16)
+                    k = part[:, t * HALF + 128 : t * HALF + HALF]
+                    v = part[:, 2 * HALF + t * 128 : 2 * HALF + t * 128 + 128]
+                    st = dot(split_heads(k, left), q, 1, 1)
+                    vt = v.T
+                    cs = []
+                    for h in range(2):
+                        s = jnp.where(live_key, st[h * sp : (h + 1) * sp], NEG)
+                        e = jnp.exp(s - jnp.max(s, axis=0, keepdims=True))
+                        p = (e * (1.0 / jnp.sum(e, axis=0, keepdims=True))).astype(BF16)
+                        p_s[g, i * pair + a, t, h] = jnp.concatenate([p, jnp.zeros((sp, LANES - sp), BF16)], axis=1)
+                        cs.append(dot(vt[h * HEAD_DIM : (h + 1) * HEAD_DIM], p, 1, 0))
+                    c2 = jnp.concatenate(cs, axis=0).T.astype(BF16)
+                    ctx_s[g, pl.ds(pl.multiple_of(i * tr + a * sp, 16), sp), t * 128 : (t + 1) * 128] = c2
+            pltpu.make_async_copy(qkv_s.at[g, r], qkv_hbm.at[g, r], out_sem.at[0, g, i]).start()
+            pltpu.make_async_copy(ctx_s.at[g, r], ctx_hbm.at[g, r], out_sem.at[1, g, i]).start()
+            im = pl.ds(i * pair, pair)
+            pltpu.make_async_copy(p_s.at[g, im], p_hbm.at[g, im], out_sem.at[2, g, i]).start()
+            return 0
+
+        lax.fori_loop(0, tiles, tile, 0)
+        pltpu.make_async_copy(watt.at[g], watt_hbm.at[g], in_sem.at[2 + g]).start()
+        return 0
+
+    lax.fori_loop(0, groups, group, 0)
+
+    def project_out(i, _):
+        run_slot(plan, "out", (i,))
+        r = pl.ds(pl.multiple_of(i * tr, 16), tr)
+        w = jnp.concatenate([out_columns(matrix(watt.at[g, 1])) for g in range(groups)], axis=1)
+        c = jnp.concatenate([ctx_s[g, r, :] for g in range(groups)], axis=1)
+        attn = dot(c, w, 1, 1)
+        for a in range(pair):
+            store_columns(mid_s, pl.ds(i * pair + a, seq, stride=images), attn[a * sp : a * sp + seq])
+        return 0
+
+    lax.fori_loop(0, tiles, project_out, 0)
+
+    def residual(j, _):
+        r = pl.ds(pl.multiple_of(j * block, 16), block)
+        store_columns(mid_s, r, load_columns(mid_s, r) + x_s[r, :].astype(F32) + bout_ref[0:1, :])
+        pltpu.make_async_copy(mid_s.at[:, r], mid_hbm.at[:, r], out_sem.at[3, 0, j]).start()
+        return 0
+
+    lax.fori_loop(0, 7, residual, 0)
+
+    def drain(k, _):
+        g, i = k // tiles, lax.rem(k, tiles)
+        r = pl.ds(pl.multiple_of(i * tr, 16), tr)
+        pltpu.make_async_copy(qkv_s.at[g, r], qkv_hbm.at[g, r], out_sem.at[0, g, i]).wait()
+        pltpu.make_async_copy(ctx_s.at[g, r], ctx_hbm.at[g, r], out_sem.at[1, g, i]).wait()
+        im = pl.ds(i * pair, pair)
+        pltpu.make_async_copy(p_s.at[g, im], p_hbm.at[g, im], out_sem.at[2, g, i]).wait()
+        return 0
+
+    lax.fori_loop(0, groups * tiles, drain, 0)
+    for g in range(groups):
+        pltpu.make_async_copy(watt.at[g], watt_hbm.at[g], in_sem.at[2 + g]).wait()
+    for j in range(7):
+        r = pl.ds(j * block, block)
+        pltpu.make_async_copy(mid_s.at[:, r], mid_hbm.at[:, r], out_sem.at[3, 0, j]).wait()
+    late.wait()
+
+
+def feed_forward_kernel(
+    dims,
+    counts_ref, norm_ref, bout_ref, bias_ref, mid_hbm, og_hbm, wff_hbm, own_hbm,
+    bo_hbm, dmid_hbm, late_hbm, sums_ref, b1g_ref, gff_ref,
+    wff, own, h2, h2t, dm, dmt, mlp, dh2, act, dpre, grad, mid_s,
+    r0, r1a, r1b, r2, r3, rs_send, rs_recv,
+    ag_send, ag_recv, ag_local, in_sem, mid_sem, out_sem,
+):
+    images, seq, sp, chunks, early, summed = dims
+    rows = images * seq
+    padded = h2.shape[0]
+    block = rows // 7
+    at = Place()
+    og_copy = pltpu.make_async_copy(og_hbm, dm.at[pl.ds(0, rows)], in_sem.at[0])
+    own_copy = pltpu.make_async_copy(own_hbm, own, in_sem.at[1])
+    w_copies = [pltpu.make_async_copy(wff_hbm.at[f], wff.at[f], in_sem.at[2 + f]) for f in range(early)]
+    own_copy.start()
+    og_copy.start()
+
+    def mid_copy(i):
+        r = pl.ds(pl.multiple_of(i * block, 16), block)
+        return pltpu.make_async_copy(mid_hbm.at[:, r], mid_s.at[lax.rem(i, 3)], mid_sem.at[lax.rem(i, 3)])
+
+    mid_copy(0).start()
+    start_all(w_copies)
+    late = chunks - early
+    gather = {
+        early + k: gather_both(
+            at, wff.at[early + k], own.at[k], (ag_send.at[k], ag_recv.at[k], ag_local.at[k])
+        )
+        for k in range(late)
+    }
+    scratch = (r0, r1a, r1b, r2, r3, rs_send, rs_recv)
+    scatter = [
+        scatter_both(
+            at, k, (grad.at[k % 2, 0], grad.at[k % 2, 1]), scratch, (gff_ref.at[k, 0], gff_ref.at[k, 1])
+        )
+        for k in range(summed)
+    ]
+    at.barrier()
+    own_copy.wait()
+    gather[early][0]()
+    og_copy.wait()
+    count = counts_ref[0]
+
+    first = at.x * images
+    image = lax.rem(lax.broadcasted_iota(jnp.int32, (block, 1), 0), images) + first
+    live = jnp.where(image < count, 1.0, 0.0).astype(F32)
+
+    def second_norm(i, _):
+        pl.when(i + 1 < 7)(lambda: mid_copy(i + 1).start())
+        mid_copy(i).wait()
+        r = pl.ds(pl.multiple_of(i * block, 16), block)
+        xhat, _r = normed(load_columns(mid_s.at[lax.rem(i, 3)], slice(None)))
+        h2[r, :] = (xhat * norm_ref[2:3, :] + norm_ref[3:4, :]).astype(BF16)
+        dm[r, :] = (dm[r, :].astype(F32) * live).astype(BF16)
+        mlp[r, :] = jnp.zeros((block, mlp.shape[1]), F32)
+        dh2[r, :] = jnp.zeros((block, mlp.shape[1]), F32)
+        return 0
+
+    rest = pl.ds(rows, padded - rows)
+    for ref in (h2, dm, act, dpre):
+        ref[rest, :] = jnp.zeros((padded - rows, ref.shape[1]), BF16)
+    lax.fori_loop(0, 7, second_norm, 0)
+    gather[early][1]()
+    gather[early + 1][0]()
+
+    def turn(j, _):
+        r = pl.ds(pl.multiple_of(j * 128, 128), 128)
+        h2t[:, r] = h2[r, :].T
+        dmt[:, r] = dm[r, :].T
+        return 0
+
+    lax.fori_loop(0, padded // 128, turn, 0)
+    wait_all(w_copies)
+
+    entries = []
+    for k in range(late):
+        first = 4 * (early + k)
+        slots = [max(0, first - 11), max(0, first - 8), first - 6, first - 3, first]
+        for s in range(5):
+            if not (k == 0 and s < 2) and not (k == 1 and s < 1):
+                entries.append((slots[s], gather[early + k][s]))
+    for k in range(summed):
+        for s, lag in enumerate((4, 6, 8, 10, 13)):
+            entries.append((4 * k + lag, scatter[k][s]))
+    entries.sort(key=lambda e: e[0])
+    plan = planned([(slot % 4, (slot // 4,), step) for slot, step in entries if slot < 4 * chunks])
+    tail = [step for slot, step in entries if slot >= 4 * chunks]
+
+    def chunk(f, _):
+        b1 = bias_ref[f]
+        for i in range(2):
+            run_slot(plan, i, (f,))
+            r = pl.ds(i * (rows // 2), rows // 2)
+            w1, w2 = matrix(wff.at[f, 0]), matrix(wff.at[f, 1])
+            pre = dot(h2[r, :], w1, 1, 0) + b1
+            phi = 0.5 + 0.5 * lax.erf(pre * 0.7071067811865476)
+            a = (pre * phi).astype(BF16)
+            slope = phi + pre * (jnp.exp(-0.5 * pre * pre) * 0.3989422804014327)
+            d = (dot(dm[r, :], w2, 1, 0) * slope).astype(BF16)
+            act[r, :] = a
+            dpre[r, :] = d
+            mlp[r, :] += dot(a, w2, 1, 1)
+            dh2[r, :] += dot(d, w1, 1, 1)
+        slot = lax.rem(f, 2)
+        shape = grad.shape[2:]
+        run_slot(plan, 2, (f,))
+        b1g_ref[f] = jnp.sum(dpre[...].astype(F32), axis=0, keepdims=True)
+        grad[slot, 0] = dot(h2t[...], dpre[...], 1, 0).astype(BF16).reshape(shape)
+        run_slot(plan, 3, (f,))
+        grad[slot, 1] = dot(dmt[...], act[...], 1, 0).astype(BF16).reshape(shape)
+
+        def keep(k):
+            pltpu.make_async_copy(grad.at[k % 2], late_hbm.at[k - summed], out_sem.at[k - summed]).start()
+
+        for k in range(summed, chunks):
+            pl.when(f == k)(functools.partial(keep, k))
+        return 0
+
+    lax.fori_loop(0, chunks, chunk, 0)
+    mid_copy(0).start()
+
+    def dmid_copy(i):
+        r = pl.ds(pl.multiple_of(i * block, 16), block)
+        return pltpu.make_async_copy(mid_s.at[lax.rem(i, 3)], dmid_hbm.at[:, r], out_sem.at[16 + lax.rem(i, 3)])
+
+    def second_norm_back(i, acc):
+        pl.when(i >= 2)(lambda: dmid_copy(i - 2).wait())
+        pl.when(i + 1 < 7)(lambda: mid_copy(i + 1).start())
+        mid_copy(i).wait()
+        r = pl.ds(pl.multiple_of(i * block, 16), block)
+        mid = load_columns(mid_s.at[lax.rem(i, 3)], slice(None))
+        xhat, rstd = normed(mid)
+        h2[r, :] = (mid + mlp[r, :] + bout_ref[1:2, :]).astype(BF16)
+        e = dh2[r, :]
+        live = dm[r, :].astype(F32)
+        d = live + norm_back(e, norm_ref[2:3, :], xhat, rstd)
+        store_columns(mid_s.at[lax.rem(i, 3)], slice(None), d)
+        pltpu.make_async_copy(h2.at[r], bo_hbm.at[r], out_sem.at[8 + i]).start()
+        dmid_copy(i).start()
+        terms = (e * xhat, e, d, live)
+        return tuple(a + jnp.sum(t, axis=0, keepdims=True) for a, t in zip(acc, terms))
+
+    zero = jnp.zeros((1, mlp.shape[1]), F32)
+    acc = lax.fori_loop(0, 7, second_norm_back, (zero,) * 4)
+    sums_ref[...] = jnp.zeros(sums_ref.shape, F32)
+    for k in range(4):
+        sums_ref[k : k + 1, :] = acc[k]
+    for step in tail:
+        step()
+
+    for i in range(7):
+        r = pl.ds(i * block, block)
+        pltpu.make_async_copy(h2.at[r], bo_hbm.at[r], out_sem.at[8 + i]).wait()
+    dmid_copy(5).wait()
+    dmid_copy(6).wait()
+    for k in range(summed, chunks):
+        pltpu.make_async_copy(grad.at[k % 2], late_hbm.at[k - summed], out_sem.at[k - summed]).wait()
+
+
+def attention_back_kernel(
+    dims,
+    norm_ref, sums_ref, b1g_ref, x_hbm, dmid_hbm, late_hbm, watt_hbm, qkv_hbm, ctx_hbm, p_hbm,
+    gt_hbm, glate_ref, gatt_ref, small_ref,
+    dattn, h1t, dh1, dqkv, watt, qkv_s, ctx_s, ctxt, p_s, grad, x_s, dmid_s, gt_s, bias_s,
+    small, small_z,
+    r0, r1a, r1b, r2, r3, rs_send, rs_recv, sm_send, sm_recv,
+    in_sem, ctx_sem, tile_sem, dmid_sem, gt_sem,
+):
+    images, seq, sp, groups, chunks, held = dims
+    rows = images * seq
+    block = rows // 7
+    model = x_s.shape[1]
+    pair = 2
+    tr = pair * sp
+    tiles = images // pair
+    at = Place()
+    dmid_in = pltpu.make_async_copy(dmid_hbm, dh1, in_sem.at[0])
+    watt_copy = pltpu.make_async_copy(watt_hbm, watt, in_sem.at[1])
+    x_copy = pltpu.make_async_copy(x_hbm, x_s, in_sem.at[2])
+    late_copies = [pltpu.make_async_copy(late_hbm.at[k], grad.at[k], in_sem.at[3 + k]) for k in range(held)]
+
+    def dmid_copy(i):
+        r = pl.ds(pl.multiple_of(i * block, 16), block)
+        return pltpu.make_async_copy(dmid_hbm.at[:, r], dmid_s.at[lax.rem(i, 2)], dmid_sem.at[lax.rem(i, 2)])
+
+    def ctx_copy(g):
+        return pltpu.make_async_copy(ctx_hbm.at[g], ctx_s.at[lax.rem(g, 2)], ctx_sem.at[lax.rem(g, 2)])
+
+    def tile_copies(g, i):
+        r, im = pl.ds(pl.multiple_of(i * tr, 16), tr), pl.ds(i * pair, pair)
+        return [
+            pltpu.make_async_copy(qkv_hbm.at[g, r], qkv_s.at[r], tile_sem.at[0, i]),
+            pltpu.make_async_copy(p_hbm.at[g, im], p_s.at[im], tile_sem.at[1, i]),
+        ]
+
+    late_copies[0].start()
+    dmid_in.start()
+    x_copy.start()
+    watt_copy.start()
+    start_all(late_copies[1:])
+    ctx_copy(0).start()
+    for i in range(tiles):
+        start_all(tile_copies(0, i))
+    scratch = (r0, r1a, r1b, r2, r3, rs_send, rs_recv)
+    scatter = [
+        scatter_both(at, k, (grad.at[k, 0], grad.at[k, 1]), scratch, (glate_ref.at[k, 0], glate_ref.at[k, 1]))
+        for k in range(held)
+    ]
+    for g in range(groups):
+        scatter.append(
+            scatter_both(
+                at, held + g, (grad.at[(held + g) % 2, 0], grad.at[(held + g) % 2, 1]), scratch, (gatt_ref.at[g, 0], gatt_ref.at[g, 1])
+            )
+        )
+    own_z = small_z.at[at.z]
+    sm = [
+        remote(small.at[0], small.at[1], sm_send.at[0], sm_recv.at[0], at.sib),
+        remote(small.at[2], small.at[3], sm_send.at[1], sm_recv.at[1], at.peer_x),
+        remote(small.at[4], small.at[5], sm_send.at[2], sm_recv.at[2], at.peer_y),
+    ]
+    sm_z = [remote(own_z, own_z, sm_send.at[3 + d], sm_recv.at[3 + d], at.peers_z[d]) for d in range(NZ - 1)]
+    at.barrier()
+    late_copies[0].wait()
+    scatter[0][0]()
+
+    dmid_in.wait()
+
+    def take_dattn(i, _):
+        d = pad_rows(load_columns(dh1, pl.ds(i, seq, stride=images)), sp)
+        dattn[pl.ds(pl.multiple_of(i * sp, 16), sp), :] = d.astype(BF16)
+        return 0
+
+    lax.fori_loop(0, images, take_dattn, 0)
+    x_copy.wait()
+
+    def first_norm(j, _):
+        r = pl.ds(pl.multiple_of(j * block, 16), block)
+        xhat, _r = normed(x_s[r, :].astype(F32))
+        store_columns(dh1, r, xhat * norm_ref[0:1, :] + norm_ref[1:2, :])
+        return 0
+
+    lax.fori_loop(0, 7, first_norm, 0)
+
+    def by_image(i, _):
+        h = pad_rows(load_columns(dh1, pl.ds(i, seq, stride=images)), sp)
+        dqkv[pl.ds(pl.multiple_of(i * sp, 16), sp), :] = h.astype(BF16)
+        return 0
+
+    lax.fori_loop(0, images, by_image, 0)
+
+    def turn(j, _):
+        r = pl.ds(pl.multiple_of(j * 128, 128), 128)
+        h1t[:, r] = dqkv[r, :].T
+        return 0
+
+    lax.fori_loop(0, images * sp // 128, turn, 0)
+    dh1[...] = jnp.zeros(dh1.shape, F32)
+    watt_copy.wait()
+    wait_all(late_copies[1:])
+
+    entries = [(s, scatter[0][k]) for k, s in ((1, 0), (2, 2), (3, 4), (4, 7))]
+    for j in range(1, held):
+        entries += [(2 + s, scatter[j][k]) for k, s in enumerate((0, 2, 4, 6, 9))]
+    for g in range(groups - 1):
+        entries += [(6 * (g + 1) + s, scatter[held + g][k]) for k, s in enumerate((0, 1, 3, 5, 7))]
+    last = scatter[held + groups - 1]
+    entries.sort(key=lambda e: e[0])
+    plan = planned(
+        [("tile" if s % 6 < 4 else s % 6, (s // 6, s % 6) if s % 6 < 4 else (s // 6,), step)
+         for s, step in entries if s < 6 * groups]
+    )
+    tail = [step for s, step in entries if s >= 6 * groups]
+
+    left = left_half(sp)
+    scale = HEAD_DIM ** (-0.5)
+
+    def group(g, _):
+        pl.when(g + 1 < groups)(lambda: ctx_copy(g + 1).start())
+        slot = lax.rem(g, 2)
+        keep = lax.rem(held + g, 2)
+
+        def tile(i, acc):
+            wait_all(tile_copies(g, i))
+            run_slot(plan, "tile", (g, i))
+            r = pl.ds(pl.multiple_of(i * tr, 16), tr)
+            wa, wb = matrix(watt.at[g, 0]), matrix(watt.at[g, 1])
+            dc = dot(dattn[r, :], out_columns(wb), 1, 0).astype(BF16)
+            qkv = qkv_s[r, :]
+            blocks = []
+            for a in range(pair):
+                part = qkv[a * sp : (a + 1) * sp]
+                dqs, dks, dvs = [], [], []
+                for t in range(NTP):
+                    q = part[:, t * HALF : t * HALF + 128] * jnp.asarray(scale, BF16)
+                    k = part[:, t * HALF + 128 : t * HALF + HALF]
+                    v = part[:, 2 * HALF + t * 128 : 2 * HALF + t * 128 + 128]
+                    dcx = dc[a * sp : (a + 1) * sp, t * 128 : (t + 1) * 128]
+                    dp = dot(split_heads(v, left), dcx, 1, 1)
+                    kt = k.T
+                    dqt, ds, ps = [], [], []
+                    for h in range(2):
+                        low = p_s[i * pair + a, t, h][:, :sp]
+                        p = low.astype(F32)
+                        pd = p * dp[h * sp : (h + 1) * sp]
+                        s = (pd - p * jnp.sum(pd, axis=0, keepdims=True)).astype(BF16)
+                        ds.append(s)
+                        ps.append(low)
+                        dqt.append(dot(kt[h * HEAD_DIM : (h + 1) * HEAD_DIM], s, 1, 0))
+                    dqs.append(jnp.concatenate(dqt, axis=0).T * scale)
+                    dk = dot(jnp.concatenate(ds, axis=0), q, 1, 0)
+                    dks.append(jnp.where(left, dk[:sp], dk[sp:]))
+                    dv = dot(jnp.concatenate(ps, axis=0), dcx, 1, 0)
+                    dvs.append(jnp.where(left, dv[:sp], dv[sp:]))
+                blocks.append(jnp.concatenate([dqs[0], dks[0], dqs[1], dks[1], dvs[0], dvs[1]], axis=1))
+            d = jnp.concatenate(blocks, axis=0).astype(BF16)
+            dqkv[r, :] = d
+            back = dot(d, projection(wa, wb), 1, 1)
+            for a in range(pair):
+                mine = pl.ds(i * pair + a, seq, stride=images)
+                store_columns(dh1, mine, load_columns(dh1, mine) + back[a * sp : a * sp + seq])
+            pl.when(g + 1 < groups)(lambda: start_all(tile_copies(g + 1, i)))
+            return acc + jnp.sum(d.astype(F32), axis=0, keepdims=True)
+
+        ctx_copy(g).wait()
+        ctxt[...] = ctx_s[slot].T
+        bias_s[g] = lax.fori_loop(0, images // pair, tile, jnp.zeros((1, model), F32))
+        run_slot(plan, 4, (g,))
+        shape = grad.shape[2:]
+        gw = dot(h1t[...], dqkv[...], 1, 0).astype(BF16)
+        grad[keep, 0] = gw[:, : 2 * HALF].reshape(shape)
+        run_slot(plan, 5, (g,))
+        go = dot(ctxt[...], dattn[...], 1, 0).T.astype(BF16)
+        grad[keep, 1] = jnp.concatenate(
+            [gw[:, 2 * HALF : 2 * HALF + 128], go[:, :128], gw[:, 2 * HALF + 128 :], go[:, 128:]], axis=1
+        ).reshape(shape)
+        return 0
+
+    lax.fori_loop(0, groups, group, 0)
+    last[0]()
+    dmid_copy(0).start()
+
+    def first_norm_back(i, acc):
+        pl.when(i + 1 < 7)(lambda: dmid_copy(i + 1).start())
+        dmid_copy(i).wait()
+        r = pl.ds(pl.multiple_of(i * block, 16), block)
+        xhat, rstd = normed(x_s[r, :].astype(F32))
+        e = load_columns(dh1, r)
+        d = load_columns(dmid_s.at[lax.rem(i, 2)], slice(None))
+        gt_s[i] = d + norm_back(e, norm_ref[0:1, :], xhat, rstd)
+        pltpu.make_async_copy(gt_s.at[i], gt_hbm.at[r], gt_sem.at[i]).start()
+        return (acc[0] + jnp.sum(e * xhat, axis=0, keepdims=True), acc[1] + jnp.sum(e, axis=0, keepdims=True))
+
+    zero = jnp.zeros((1, model), F32)
+    acc = lax.fori_loop(0, 4, first_norm_back, (zero, zero))
+    for step in tail:
+        step()
+    last[1]()
+    acc = lax.fori_loop(4, 7, first_norm_back, acc)
+    small[0] = jnp.zeros(small.shape[1:], F32)
+    small[0, 0:1, :] = acc[0]
+    small[0, 1:2, :] = acc[1]
+    small[0, 2:6, :] = sums_ref[0:4, :]
+    own_cols = groups * 128
+    for g in range(groups):
+        for t in range(NTP):
+            cols = slice(t * own_cols + 128 * g, t * own_cols + 128 * g + 128)
+            small[0, 6:7, cols] = bias_s[g, :, t * HALF : t * HALF + 128]
+            small[0, 7:8, cols] = bias_s[g, :, 2 * HALF + t * 128 : 2 * HALF + t * 128 + 128]
+    for f in range(chunks):
+        for t in range(NTP):
+            first = t * chunks * HALF + f * HALF
+            row, col = 8 + first // model, first % model
+            small[0, row : row + 1, col : col + HALF] = b1g_ref[f, :, t * HALF : t * HALF + HALF]
+    sm[0].start()
+    last[2]()
+    sm[0].wait()
+    small[2] = small[0] + small[1]
+    sm[1].start()
+    last[3]()
+    sm[1].wait()
+    small[4] = small[2] + small[3]
+    sm[2].start()
+    last[4]()
+    sm[2].wait()
+    small_z[at.z] = small[4] + small[5]
+    start_all(sm_z)
+    for i in range(7):
+        r = pl.ds(i * block, block)
+        pltpu.make_async_copy(gt_s.at[i], gt_hbm.at[r], gt_sem.at[i]).wait()
+    wait_all(sm_z)
+    total = small_z[0]
+    for k in range(1, NZ):
+        total = total + small_z[k]
+    small_ref[...] = total
+
+
+def step_kernel(dims, *refs):
+    groups, chunks, held = dims
+    names = ("norm", "qkv", "bqv", "out", "fc1", "bfc1", "fc2", "bout")
+    gff_ref, glate_ref, gatt_ref, small_ref = refs[:4]
+    n = len(names)
+    ps, ms, vs = (dict(zip(names, refs[4 + k * n : 4 + (k + 1) * n])) for k in range(3))
+    outs = refs[4 + 3 * n :]
+    g_out, u_out, m_out, v_out = (dict(zip(names, outs[k * n : (k + 1) * n])) for k in range(4))
+    late = chunks - held
+
+    def ff(f, h):
+        return gff_ref[f, h] if f < late else glate_ref[f - late, h]
+
+    whole = {"qkv": True, "fc1": True, "fc2": True}
+    decays = ("qkv", "out", "fc1", "fc2")
+
+    def update(name, index, g):
+        p = ps[name][index]
+        u, m, v = adamw(p, g, ms[name][index], vs[name][index], decay_rate if name in decays else 0.0)
+        g_out[name][index] = g
+        u_out[name][index] = p + u if name in whole else u
+        m_out[name][index] = m
+        v_out[name][index] = v
+
+    for c in range(3):
+        gs = [gatt_ref[g, c // 2][:, (c % 2) * 128 : (c % 2) * 128 + 128] for g in range(groups)]
+        update("qkv", c, jnp.concatenate(gs, axis=1))
+    update("out", ..., jnp.concatenate([gatt_ref[g, 1][:, 128:] for g in range(groups)], axis=1))
+    for f in range(chunks):
+        cols = slice(f * HALF, (f + 1) * HALF)
+        update("fc1", (slice(None), cols), ff(f, 0))
+        update("fc2", (slice(None), cols), ff(f, 1))
+    update("norm", ..., small_ref[0:4, :])
+    update("bout", ..., small_ref[4:6, :])
+    part = lax.axis_index("tp") * (NZ * NY * NCORE) + lax.axis_index("fsdp")
+    width = ps["bqv"].shape[1]
+    model = small_ref.shape[1]
+    update("bqv", ..., pltpu.roll(small_ref[0:8, :], lax.rem(model - part * width, model), 1)[6:8, :width])
+    width = ps["bfc1"].shape[1]
+    per = model // width
+    turned = pltpu.roll(small_ref[8:16, :], lax.rem(model - lax.rem(part, per) * width, model), 1)[:, :width]
+    at_row = lax.broadcasted_iota(jnp.int32, turned.shape, 0)
+    update("bfc1", ..., jnp.sum(jnp.where(at_row == part // per, turned, 0.0), axis=0, keepdims=True))
+
+
+def sds(shape, dtype):
+    return jax.ShapeDtypeStruct(shape, dtype)
+
+
+def fused_device(
+    tokens_in, out_grad, image_counts,
+    norm_params, w_qkv, bias_qv, w_out, w_fc1, bias_fc1, w_fc2, bias_out,
+    *moments,
+):
+    images, seq, model = tokens_in.shape
+    sp = -(-seq // 16) * 16
+    rows = images * sp
+    own_rows, own_cols = w_qkv.shape[1], w_qkv.shape[2]
+    groups = own_cols // 128
+    chunks = w_fc1.shape[1] // HALF
+    early, summed = 2, chunks - 2
+    held = chunks - summed
+    wide = NTP * HALF
+    cube = (NZ, NY, NCORE, own_rows, wide)
+    any_, vm, sm = pl.BlockSpec(memory_space=pl.ANY), pl.BlockSpec(memory_space=pltpu.VMEM), pl.BlockSpec(memory_space=pltpu.SMEM)
+    dma = pltpu.SemaphoreType.DMA
+
+    def params(k):
+        return pltpu.CompilerParams(collective_id=k, has_side_effects=True, vmem_limit_bytes=VMEM_BYTES)
+
+    n_ag = groups + early
+    flat_rows = images * seq
+
+    def by_token(a):
+        return a.transpose(1, 0, 2).reshape(flat_rows, model)
+
+    def by_image(a):
+        return a.reshape(seq, images, model).transpose(1, 0, 2)
+
+    x_rows, og_rows = by_token(tokens_in), by_token(out_grad)
+    qkv, ctx, mid, p, watt, wff, own, bias1 = pl.pallas_call(
+        functools.partial(attention_kernel, (images, seq, sp, groups, groups + chunks, early)),
+        name="attention",
+        in_specs=[any_] + [vm] * 8,
+        out_specs=[any_] * 7 + [vm],
+        out_shape=[
+            sds((groups, rows, model), BF16), sds((groups, rows, HALF), BF16), sds((model // 128, flat_rows, 128), F32),
+            sds((groups, images, NTP, 2, sp, LANES), BF16), sds((groups, 2) + cube, BF16), sds((early, 2) + cube, BF16),
+            sds((chunks - early, 2, own_rows, HALF), BF16), sds((chunks, 1, wide), F32),
+        ],
+        scratch_shapes=[
+            pltpu.VMEM((flat_rows, model), BF16), pltpu.VMEM((rows, model), BF16),
+            pltpu.VMEM((groups, rows, model), BF16), pltpu.VMEM((groups, rows, HALF), BF16),
+            pltpu.VMEM((model // 128, flat_rows, 128), F32), pltpu.VMEM((groups, images, NTP, 2, sp, LANES), BF16),
+            pltpu.VMEM((groups, 2) + cube, BF16), pltpu.VMEM((groups + chunks, 2, own_rows, HALF), BF16),
+            pltpu.VMEM((NTP, NZ, NY, NCORE, 8, 128), F32), pltpu.VMEM((groups, 1, model), F32),
+            dma((n_ag, 2, AG_SEMS)), dma((n_ag, 2, AG_SEMS)), dma((n_ag, 2)), dma((6,)), dma((6,)),
+            dma((4, groups, 8)), dma((2 + groups,)),
+        ],
+        compiler_params=params(0),
+    )(x_rows, norm_params, bias_out, w_qkv, w_out.T, w_fc1, w_fc2.T, bias_qv, bias_fc1.reshape(1, -1))
+
+    late = chunks - early
+    bo, dmid, grad_late, sums, b1g, gff = pl.pallas_call(
+        functools.partial(feed_forward_kernel, (images, seq, sp, chunks, early, summed)),
+        name="feed_forward",
+        in_specs=[sm, vm, vm, vm] + [any_] * 4,
+        out_specs=[any_] * 3 + [vm] * 3,
+        out_shape=[
+            sds((flat_rows, model), BF16), sds((model // 128, flat_rows, 128), F32),
+            sds((held, 2) + cube, BF16), sds((8, model), F32), sds((chunks, 1, wide), F32),
+            sds((summed, 2, own_rows, HALF), F32),
+        ],
+        scratch_shapes=[
+            pltpu.VMEM((chunks, 2) + cube, BF16), pltpu.VMEM((late, 2, own_rows, HALF), BF16),
+            pltpu.VMEM((rows, model), BF16), pltpu.VMEM((model, rows), BF16),
+            pltpu.VMEM((rows, model), BF16), pltpu.VMEM((model, rows), BF16),
+            pltpu.VMEM((flat_rows, model), F32), pltpu.VMEM((flat_rows, model), F32),
+            pltpu.VMEM((rows, wide), BF16), pltpu.VMEM((rows, wide), BF16),
+            pltpu.VMEM((2, 2) + cube, BF16), pltpu.VMEM((3, model // 128, flat_rows // 7, 128), F32),
+        ]
+        + scatter_scratch(summed, own_rows)
+        + [
+            dma((late, 2, AG_SEMS)), dma((late, 2, AG_SEMS)), dma((late, 2)), dma((2 + early,)), dma((3,)),
+            dma((24,)),
+        ],
+        compiler_params=params(1),
+    )(image_counts, norm_params, bias_out, bias1, mid, og_rows, wff, own)
+
+    gt, glate, gatt, small = pl.pallas_call(
+        functools.partial(attention_back_kernel, (images, seq, sp, groups, chunks, held)),
+        name="attention_back",
+        in_specs=[vm] * 3 + [any_] * 7,
+        out_specs=[any_] + [vm] * 3,
+        out_shape=[
+            sds((flat_rows, model), F32), sds((held, 2, own_rows, HALF), F32),
+            sds((groups, 2, own_rows, HALF), F32), sds((16, model), F32),
+        ],
+        scratch_shapes=[
+            pltpu.VMEM((rows, model), BF16), pltpu.VMEM((model, rows), BF16),
+            pltpu.VMEM((model // 128, flat_rows, 128), F32), pltpu.VMEM((rows, model), BF16),
+            pltpu.VMEM((groups, 2) + cube, BF16),
+            pltpu.VMEM((rows, model), BF16), pltpu.VMEM((2, rows, HALF), BF16), pltpu.VMEM((HALF, rows), BF16),
+            pltpu.VMEM((images, NTP, 2, sp, LANES), BF16), pltpu.VMEM((2, 2) + cube, BF16),
+            pltpu.VMEM((flat_rows, model), BF16), pltpu.VMEM((2, model // 128, flat_rows // 7, 128), F32),
+            pltpu.VMEM((7, flat_rows // 7, model), F32), pltpu.VMEM((groups, 1, model), F32),
+            pltpu.VMEM((6, 16, model), F32), pltpu.VMEM((NZ, 16, model), F32),
+        ]
+        + scatter_scratch(held + groups, own_rows)
+        + [dma((6,)), dma((6,)), dma((3 + held,)), dma((2,)), dma((2, images // 2)), dma((2,)), dma((8,))],
+        compiler_params=params(2),
+    )(norm_params, sums, b1g, x_rows, dmid, grad_late, watt, qkv, ctx, p)
+
+    turned = (3, 6)
+
+    def flat(a, k):
+        return a.reshape(1, -1) if a.ndim == 1 else a.T if k in turned else a
+
+    weights = [flat(a, k) for k, a in enumerate((norm_params, w_qkv, bias_qv, w_out, w_fc1, bias_fc1, w_fc2, bias_out))]
+    moments = [flat(a, k % 8) for k, a in enumerate(moments)]
+    shapes = [sds(a.shape, F32) for a in weights]
+    outs = pl.pallas_call(
+        functools.partial(step_kernel, (groups, chunks, held)),
+        name="adamw_step",
+        in_specs=[vm] * 28,
+        out_specs=[vm] * 32,
+        out_shape=shapes * 4,
+        compiler_params=pltpu.CompilerParams(vmem_limit_bytes=VMEM_BYTES),
+    )(gff, glate, gatt, small, *weights, *moments)
+    outs = [o.reshape(-1) if k % 8 == 5 else o.T if k % 8 in turned else o for k, o in enumerate(outs)]
+    return (by_image(bo), by_image(gt)) + tuple(outs)
+
+
 def solution(mesh):
     placed = (
         P(("fsdp", "tp"), None, None),
@@ -276,8 +1322,9 @@
         P("tp", "fsdp"),
         P(),
     )
+    fits = mesh.shape["fsdp"] == NZ * NY * NCORE and mesh.shape["tp"] == NTP
     return jax.shard_map(
-        per_device,
+        fused_device if fits else per_device,
         mesh=mesh,
         in_specs=placed,
         out_specs=(

time: 1010 us -> 266 us (0.26); the launches traced: 998 us -> 266 us
  waiting for transfers between devices: 375 us -> 0 us
  Pallas kernels: 0 us -> 259 us
  matrix products: 230 us -> 0 us
  blocking collectives: 177 us -> 0 us
  other arithmetic: 112 us -> 0 us
  local copies, waits for them, and re-layouts: 85.6 us -> 5.7 us
  between operations: 18.4 us -> 1.37 us
    pallas_call x0 -> x4, Pallas kernels: none -> 259 us  [the longest x1 97.9 us: fused_device(): pl.pallas_call(functools.partial(feed_forward_kernel, (images, seq, sp, c...]
    dot_general x18 -> x0, matrix products: 230 us -> none  [the longest x1 29.5 us: per_device(): jnp.einsum('gsd,fd->gsf', grad_mlp_in, fc2_use, preferred_element_type=jn...]
    reduce_scatter x6 -> x0, waiting for transfers between devices: 187 us -> none  [the longest x1 75.6 us: per_device(): lax.psum_scatter(grad_w2, 'fsdp', scatter_dimension=1, tiled=True)]
    all_gather x7 -> x0, waiting for transfers between devices: 114 us -> none  [the longest x1 45 us: per_device(): lax.all_gather(w_qkv.astype(jnp.bfloat16), 'fsdp', axis=1, tiled=True)]
    unnamed x2 -> x0, blocking collectives: 94.8 us -> none
    unnamed x19 -> x0, waiting for transfers between devices: 73 us -> none
    convert_element_type x11 -> x0, other arithmetic: 64.4 us -> none  [the longest x1 45.1 us: per_device(): activated = exact_gelu(pre_act).astype(jnp.bfloat16)]
    all_gather x3 -> x0, blocking collectives: 42.6 us -> none  [the longest x1 20.9 us: per_device(): lax.all_gather(w_out.astype(jnp.bfloat16), 'fsdp', axis=1, tiled=True)]
  transfers between devices with their start and end apart: 16 -> 0, of which waited for: 9 -> 0; matrix products, arithmetic and copies ran while one was open for 35% -> 0% of each run, Pallas kernels for 0% -> 0%
where the time goes in v1:
time: 266 us
  Pallas kernels  259 us (97%)
  local copies, waits for them, and re-layouts  5.7 us (2%)
    pallas_call x1, Pallas kernels, fused_device(): pl.pallas_call(functools.partial(feed_forward_kernel, (images, seq, sp, c...  97.9 us
    pallas_call x1, Pallas kernels, fused_device(): pl.pallas_call(functools.partial(attention_back_kernel, (images, seq, sp,...  87.4 us
    pallas_call x1, Pallas kernels, fused_device(): pl.pallas_call(functools.partial(attention_kernel, (images, seq, sp, grou...  69 us
    unnamed x4, local copies, waits for them, and re-layouts  5.7 us

profile of v1, /device:TPU:0, one launch (start us, length us, event | category | flops | bytes accessed | tf_op | source)
XLA Modules:
  0.0 265.8 jit_solution(18257275476625996805)
XLA Ops:
  1.3 69.0 %attention.1 = (bf16[3,1664,768]{2,1,0:T(8,128)(2,1)}, bf16[3,1664,256]{2,1,0:T(8,128)(2,1)}, f32[6,1568,128]{2,1,0:T(8,128)}, bf16[3,8,2,2,208,256]{5,4,3,2,1,0...) custom-call(bf16[1568,768]{1,0:T(8,128)(2,1)} %bitcast.33, ...), custom_call_target="tpu_custom_call" | custom-call | tf_op jit(solution)/shard_map/attention/pallas_call | solution.py:1202
  70.3 97.9 %feed_forward.1 = (bf16[1568,768]{1,0:T(8,128)(2,1)}, f32[6,1568,128]{2,1,0:T(8,128)}, bf16[2,2,4,2,2,48,512]{6,5,4,3,2,1,0:T(8,128)(2,1)}, f32[8,768]{1,0:T(8,1...) custom-call(s32[1]{0:T(128)S(6)} %copy.63.counts_ref, f32[4,768]{1,0:T(4,128)} %refs_4_.1, f32[2,768]{1,0:T(2,128)} %refs_11_.1, ...), custom_call_target="tpu_custom_call" | custom-call | tf_op jit(solution)/shard_map/feed_forward/pallas_call | solution.py:1225
  168.2 87.4 %attention_back.1 = (f32[1568,768]{1,0:T(8,128)}, f32[2,2,48,256]{3,2,1,0:T(8,128)}, f32[3,2,48,256]{3,2,1,0:T(8,128)}, f32[16,768]{1,0:T(8,128)}) custom-call(f32[4,768]{1,0:T(4,128)} %refs_4_.1, f32[8,768]{1,0:T(8,128)} %get-tuple-element.89.sums_ref, f32[6,1,512]{2,1,0:T(1,128)} %get-tuple-element.90.b1g_ref, bf16[1568,768]{1,0:T(8,128)(2,1)} %bitcast.34, ...), custom_call_target="tpu_custom_call" | custom-call | tf_op jit(solution)/shard_map/attention_back/pallas_call | solution.py:1251
  255.6 4.5 %adamw_step.1 = (f32[4,768]{1,0:T(4,128)}, f32[3,48,384]{2,1,0:T(8,128)}, f32[2,24]{1,0:T(2,128)}, f32[48,384]{1,0:T(8,128)}, f32[48,1536]{1,0:T(8,128)}, /*inde...) custom-call(f32[4,2,48,256]{3,2,1,0:T(8,128)} %get-tuple-element.98., ...), custom_call_target="tpu_custom_call" | custom-call | tf_op jit(solution)/shard_map/adamw_step/pallas_call | solution.py:1283
  260.1 0.0 copy-start
  260.1 3.4 %copy.64 = bf16[8,196,768]{2,0,1:T(8,128)(2,1)} copy(bf16[8,196,768]{2,0,1:T(8,128)(2,1)} %bitcast.36) | data formatting | bytes 4816896
  263.5 0.1 copy-done
  263.6 2.2 copy.65
Async XLA Ops:
  260.1 3.5 %copy-start = (f32[1568,768]{1,0:T(8,128)S(1)}, f32[1568,768]{1,0:T(8,128)}, u32[]{:S(2)}) copy-start(f32[1568,768]{1,0:T(8,128)} %get-tuple-element.97) | copy-start | bytes 14450692

commit v2 on v1

--- a/solution.py
+++ b/solution.py
@@ -302,6 +302,16 @@
         self.peer_y = self.at(self.z, 1 - self.y, self.c, self.x)
         self.other_z = [lax.rem(self.z + d, NZ) for d in range(1, NZ)]
         self.peers_z = [self.at(o, self.y, self.c, self.x) for o in self.other_z]
+        self.quad = 2 * self.x + self.c
+        self.quad_peers = [
+            self.at(self.z, self.y, lax.rem(self.c + k, 2), lax.rem(self.x + k // 2, 2))
+            for k in range(1, 4)
+        ]
+        self.line = self.z * NY + self.y
+        self.line_peers = []
+        for k in range(1, NZ * NY):
+            other = lax.rem(self.line + k, NZ * NY)
+            self.line_peers.append(self.at(other // NY, lax.rem(other, NY), self.c, self.x))
         self.lanes = pl.ds(pl.multiple_of(self.x * HALF, HALF), HALF)
         self.lanes_other = pl.ds(pl.multiple_of((1 - self.x) * HALF, HALF), HALF)
 
@@ -311,9 +321,9 @@
     def at(self, z, y, c, x):
         return {"fsdp": (z * NY + y) * NCORE + c, "tp": x}
 
-    def barrier(self):
+    def barrier(self, everyone=None):
         sem = pltpu.get_barrier_semaphore()
-        everyone = [self.sib, self.peer_x, self.peer_y] + self.peers_z
+        everyone = everyone or [self.sib, self.peer_x, self.peer_y] + self.peers_z
         for d in everyone:
             pl.semaphore_signal(sem, inc=1, device_id=d, device_id_type=MESH_IDS)
         pl.semaphore_wait(sem, len(everyone))
@@ -338,17 +348,18 @@
 AG_SEMS = 7
 
 
-def gather_steps(at, buf, own, send, recv, local, y_first):
+def gather_steps(at, buf, own, send, recv, local, y_first, part=slice(None)):
     x, y, z, c, lanes = at.x, at.y, at.z, at.c, at.lanes
-    mine = buf.at[z, y, c, :, lanes]
+    own = own.at[part]
+    mine = buf.at[z, y, c, part, lanes]
     keep = pltpu.make_async_copy(own, mine, local)
     s0 = [remote(own, mine, send.at[d], recv.at[d], at.peers_z[d]) for d in range(NZ - 1)]
-    line = buf.at[:, y, c, :, lanes]
+    line = buf.at[:, y, c, part, lanes]
     s1 = remote(line, line, send.at[3], recv.at[3], at.peer_y if y_first else at.peer_x)
     if y_first:
-        plane, rest = buf.at[:, :, c, :, lanes], buf.at[:, :, c, :, at.lanes_other]
+        plane, rest = buf.at[:, :, c, part, lanes], buf.at[:, :, c, part, at.lanes_other]
     else:
-        plane, rest = buf.at[:, y, c], buf.at[:, 1 - y, c]
+        plane, rest = buf.at[:, y, c, part], buf.at[:, 1 - y, c, part]
     s2 = remote(plane, plane, send.at[4], recv.at[4], at.peer_x if y_first else at.peer_y)
     sib_a = remote(plane, plane, send.at[5], recv.at[5], at.sib)
     sib_b = remote(rest, rest, send.at[6], recv.at[6], at.sib)
@@ -473,10 +484,10 @@
     return run
 
 
-def gather_both(at, buf, own, sems):
+def gather_both(at, buf, own, sems, part=slice(None)):
     send, recv, local = sems
-    first = gather_steps(at, buf.at[0], own.at[0], send.at[0], recv.at[0], local.at[0], True)
-    second = gather_steps(at, buf.at[1], own.at[1], send.at[1], recv.at[1], local.at[1], False)
+    first = gather_steps(at, buf.at[0], own.at[0], send.at[0], recv.at[0], local.at[0], True, part)
+    second = gather_steps(at, buf.at[1], own.at[1], send.at[1], recv.at[1], local.at[1], False, part)
     return [both(a, b) for a, b in zip(first, second)]
 
 
@@ -559,7 +570,12 @@
     def sems(k):
         return ag_send.at[k], ag_recv.at[k], ag_local.at[k]
 
-    steps = [gather_both(at, watt.at[g], own.at[g], sems(g)) for g in range(groups)]
+    third = own.shape[2] // 3
+    head = [
+        gather_both(at, watt.at[0], own.at[0], sems(k), pl.ds(j * third, third))
+        for j, k in enumerate((0, groups + early, groups + early + 1))
+    ]
+    steps = [[None] * 5] + [gather_both(at, watt.at[g], own.at[g], sems(g)) for g in range(1, groups)]
     steps += [gather_both(at, wff_hbm.at[f], own.at[groups + f], sems(groups + f)) for f in range(early)]
     here = pieces.at[at.x, at.z, at.y, at.c]
     line = pieces.at[at.x, :, at.y, at.c]
@@ -571,8 +587,12 @@
         for k, (r, d) in enumerate([(line, at.peer_y), (plane, at.peer_x), (cube, at.sib)])
     ]
 
+    def head_step(k):
+        for part in head:
+            part[k]()
+
     at.barrier()
-    steps[0][0]()
+    head_step(0)
     start_all(bias_steps[0])
     steps[1][0]()
     for f in range(chunks - groups):
@@ -596,20 +616,19 @@
         h1[pl.ds(pl.multiple_of(i * sp, 16), sp), :] = h.astype(BF16)
         return 0
 
-    lax.fori_loop(0, 7, first_norm, 0)
-    steps[0][1]()
+    head_step(1)
     wait_all(bias_steps[0])
     start_all(bias_steps[1])
     steps[2][0]()
-    lax.fori_loop(0, images, by_image, 0)
-    steps[0][2]()
+    lax.fori_loop(0, 7, first_norm, 0)
+    head_step(2)
     wait_all(bias_steps[1])
     start_all(bias_steps[2])
+    lax.fori_loop(0, images, by_image, 0)
     steps[1][1]()
-    steps[0][3]()
+    head_step(3)
     wait_all(bias_steps[2])
     start_all(bias_steps[3])
-    steps[1][2]()
     wait_all(bias_steps[3])
     flat = pieces[...].reshape(NTP * NZ * NY * NCORE * 8, 128)
     width = bqv_ref.shape[1]
@@ -630,50 +649,60 @@
         bias_ref[f] = jnp.concatenate(
             [bias_ff[:, t * per + f * HALF : t * per + f * HALF + HALF] for t in range(NTP)], axis=1
         )
-    steps[0][4]()
-
-    when = {1: [None, None, None, (0, 1), (1, 0)], 2: [None, (0, 1), (0, 3), (1, 1), (2, 0)]}
-    place = [[(0, 3), (1, 1), (1, 3), (2, 1), (2, 3)], [(1, 2), (2, 0), (2, 2), (3, 0), (3, 2)]]
-    for f in range(early):
-        when[groups + f] = place[f]
+    head_step(4)
+
+    when = {1: [None, None, 2, 4, 4], 2: [None, 2, 4, 8, 8]}
+    when.update({groups + f: ns for f, ns in enumerate([[0, 4, 7, 10, 13], [4, 8, 11, 14, 14]])})
+    entries = sorted((n, k, k_step) for k, ns in when.items() for k_step, n in enumerate(ns) if n is not None)
+    last = 4 * groups + 2
     plan = planned(
-        [("out" if w[0] == groups else "tile", w[1:] if w[0] == groups else w, steps[k][s])
-         for k, ws in when.items() for s, w in enumerate(ws) if w is not None]
-    )
-
-    pair = 2
-    tr = pair * sp
+        [("out", (n - 4 * groups,), steps[k][j]) if n >= 4 * groups else (n % 2, (n // 4, n % 4 // 2), steps[k][j])
+         for n, k, j in entries if n < last]
+    )
+    remains = [steps[k][j] for n, k, j in entries if n >= last]
+
+    quad = 4
+    tr = quad * sp
     left = left_half(sp)
-    live_key = lax.broadcasted_iota(jnp.int32, (sp, sp), 0) < seq
-    tiles = images // pair
+    full = seq // 16 * 16
+    live_key = lax.broadcasted_iota(jnp.int32, (sp - full, LANES), 0) < seq - full
+    tiles = images // quad
+    units = [(a, t) for a in range(quad) for t in range(NTP)]
+
+    def soften(s):
+        s = jnp.concatenate([s[:full], jnp.where(live_key, s[full:], NEG)], axis=0)
+        e = jnp.exp(s - jnp.max(s, axis=0, keepdims=True))
+        return (e * (1.0 / jnp.sum(e, axis=0, keepdims=True))).astype(BF16)
 
     def group(g, _):
         def tile(i, _):
-            run_slot(plan, "tile", (g, i))
+            run_slot(plan, 0, (g, i))
             r = pl.ds(pl.multiple_of(i * tr, 16), tr)
             w = projection(matrix(watt.at[g, 0]), matrix(watt.at[g, 1]))
-            qkv = (dot(h1[r, :], w, 1, 0) + bias_s[g]).astype(BF16)
-            qkv_s[g, r, :] = qkv
-            for a in range(pair):
-                part = qkv[a * sp : (a + 1) * sp]
-                for t in range(NTP):
-                    q = part[:, t * HALF : t * HALF + 128] * jnp.asarray(HEAD_DIM ** (-0.5), BF16)
-                    k = part[:, t * HALF + 128 : t * HALF + HALF]
-                    v = part[:, 2 * HALF + t * 128 : 2 * HALF + t * 128 + 128]
-                    st = dot(split_heads(k, left), q, 1, 1)
-                    vt = v.T
-                    cs = []
-                    for h in range(2):
-                        s = jnp.where(live_key, st[h * sp : (h + 1) * sp], NEG)
-                        e = jnp.exp(s - jnp.max(s, axis=0, keepdims=True))
-                        p = (e * (1.0 / jnp.sum(e, axis=0, keepdims=True))).astype(BF16)
-                        p_s[g, i * pair + a, t, h] = jnp.concatenate([p, jnp.zeros((sp, LANES - sp), BF16)], axis=1)
-                        cs.append(dot(vt[h * HEAD_DIM : (h + 1) * HEAD_DIM], p, 1, 0))
-                    c2 = jnp.concatenate(cs, axis=0).T.astype(BF16)
-                    ctx_s[g, pl.ds(pl.multiple_of(i * tr + a * sp, 16), sp), t * 128 : (t + 1) * 128] = c2
+            qkv_s[g, r, :] = (dot(h1[r, :], w, 1, 0) + bias_s[g]).astype(BF16)
+            run_slot(plan, 1, (g, i))
+            qkv = qkv_s[g, r, :]
+
+            def cut(a, first):
+                return qkv[a * sp : (a + 1) * sp, first : first + 128]
+
+            scores = []
+            for a, t in units:
+                q = pad_rows(cut(a, t * HALF) * jnp.asarray(HEAD_DIM ** (-0.5), BF16), LANES)
+                scores.append(dot(split_heads(cut(a, t * HALF + 128), left), q, 1, 1))
+            probs = []
+            for (a, t), s in zip(units, scores):
+                probs.append([soften(s[h * sp : (h + 1) * sp]) for h in range(2)])
+                for h in range(2):
+                    p_s[g, i * quad + a, t, h] = probs[-1][h]
+            for (a, t), p in zip(units, probs):
+                vt = cut(a, 2 * HALF + t * 128).T
+                cs = [dot(vt[h * HEAD_DIM : (h + 1) * HEAD_DIM], p[h], 1, 0) for h in range(2)]
+                mine = pl.ds(pl.multiple_of(i * tr + a * sp, 16), sp)
+                ctx_s[g, mine, t * 128 : (t + 1) * 128] = jnp.concatenate(cs, axis=0).T[:sp].astype(BF16)
             pltpu.make_async_copy(qkv_s.at[g, r], qkv_hbm.at[g, r], out_sem.at[0, g, i]).start()
             pltpu.make_async_copy(ctx_s.at[g, r], ctx_hbm.at[g, r], out_sem.at[1, g, i]).start()
-            im = pl.ds(i * pair, pair)
+            im = pl.ds(i * quad, quad)
             pltpu.make_async_copy(p_s.at[g, im], p_hbm.at[g, im], out_sem.at[2, g, i]).start()
             return 0
 
@@ -689,8 +718,8 @@
         w = jnp.concatenate([out_columns(matrix(watt.at[g, 1])) for g in range(groups)], axis=1)
         c = jnp.concatenate([ctx_s[g, r, :] for g in range(groups)], axis=1)
         attn = dot(c, w, 1, 1)
-        for a in range(pair):
-            store_columns(mid_s, pl.ds(i * pair + a, seq, stride=images), attn[a * sp : a * sp + seq])
+        for a in range(quad):
+            store_columns(mid_s, pl.ds(i * quad + a, seq, stride=images), attn[a * sp : a * sp + seq])
         return 0
 
     lax.fori_loop(0, tiles, project_out, 0)
@@ -702,13 +731,15 @@
         return 0
 
     lax.fori_loop(0, 7, residual, 0)
+    for step in remains:
+        step()
 
     def drain(k, _):
         g, i = k // tiles, lax.rem(k, tiles)
         r = pl.ds(pl.multiple_of(i * tr, 16), tr)
         pltpu.make_async_copy(qkv_s.at[g, r], qkv_hbm.at[g, r], out_sem.at[0, g, i]).wait()
         pltpu.make_async_copy(ctx_s.at[g, r], ctx_hbm.at[g, r], out_sem.at[1, g, i]).wait()
-        im = pl.ds(i * pair, pair)
+        im = pl.ds(i * quad, quad)
         pltpu.make_async_copy(p_s.at[g, im], p_hbm.at[g, im], out_sem.at[2, g, i]).wait()
         return 0
 
@@ -762,7 +793,8 @@
     ]
     at.barrier()
     own_copy.wait()
-    gather[early][0]()
+    for k in range(late):
+        gather[early + k][0]()
     og_copy.wait()
     count = counts_ref[0]
 
@@ -785,8 +817,6 @@
     for ref in (h2, dm, act, dpre):
         ref[rest, :] = jnp.zeros((padded - rows, ref.shape[1]), BF16)
     lax.fori_loop(0, 7, second_norm, 0)
-    gather[early][1]()
-    gather[early + 1][0]()
 
     def turn(j, _):
         r = pl.ds(pl.multiple_of(j * 128, 128), 128)
@@ -798,18 +828,18 @@
     wait_all(w_copies)
 
     entries = []
-    for k in range(late):
-        first = 4 * (early + k)
-        slots = [max(0, first - 11), max(0, first - 8), first - 6, first - 3, first]
-        for s in range(5):
-            if not (k == 0 and s < 2) and not (k == 1 and s < 1):
-                entries.append((slots[s], gather[early + k][s]))
-    for k in range(summed):
-        for s, lag in enumerate((4, 6, 8, 10, 13)):
-            entries.append((4 * k + lag, scatter[k][s]))
+    for k, slots in enumerate(
+        ((None, 0, 2, 6, 8), (None, 2, 6, 10, 12), (None, 4, 7, 12, 16), (None, 6, 10, 14, 20))
+    ):
+        entries += [(n, gather[early + k][j]) for j, n in enumerate(slots) if n is not None]
+    for k, slots in enumerate(((8, 10, 16, 18, 21), (12, 14, 17, 19, 23), (16, 18, 21, 23, 24))):
+        entries += [(n, scatter[k][j]) for j, n in enumerate(slots)]
     entries.sort(key=lambda e: e[0])
     plan = planned([(slot % 4, (slot // 4,), step) for slot, step in entries if slot < 4 * chunks])
     tail = [step for slot, step in entries if slot >= 4 * chunks]
+
+    def late_copy(k):
+        return pltpu.make_async_copy(grad.at[k % 2], late_hbm.at[k - summed], out_sem.at[k - summed])
 
     def chunk(f, _):
         b1 = bias_ref[f]
@@ -829,16 +859,15 @@
         slot = lax.rem(f, 2)
         shape = grad.shape[2:]
         run_slot(plan, 2, (f,))
+        for k in range(summed, chunks - 2):
+            pl.when(f == k + 2)(late_copy(k).wait)
         b1g_ref[f] = jnp.sum(dpre[...].astype(F32), axis=0, keepdims=True)
         grad[slot, 0] = dot(h2t[...], dpre[...], 1, 0).astype(BF16).reshape(shape)
         run_slot(plan, 3, (f,))
         grad[slot, 1] = dot(dmt[...], act[...], 1, 0).astype(BF16).reshape(shape)
 
-        def keep(k):
-            pltpu.make_async_copy(grad.at[k % 2], late_hbm.at[k - summed], out_sem.at[k - summed]).start()
-
         for k in range(summed, chunks):
-            pl.when(f == k)(functools.partial(keep, k))
+            pl.when(f == k)(late_copy(k).start)
         return 0
 
     lax.fori_loop(0, chunks, chunk, 0)
@@ -878,16 +907,16 @@
         pltpu.make_async_copy(h2.at[r], bo_hbm.at[r], out_sem.at[8 + i]).wait()
     dmid_copy(5).wait()
     dmid_copy(6).wait()
-    for k in range(summed, chunks):
-        pltpu.make_async_copy(grad.at[k % 2], late_hbm.at[k - summed], out_sem.at[k - summed]).wait()
+    for k in range(chunks - 2, chunks):
+        late_copy(k).wait()
 
 
 def attention_back_kernel(
     dims,
     norm_ref, sums_ref, b1g_ref, x_hbm, dmid_hbm, late_hbm, watt_hbm, qkv_hbm, ctx_hbm, p_hbm,
     gt_hbm, glate_ref, gatt_ref, small_ref,
-    dattn, h1t, dh1, dqkv, watt, qkv_s, ctx_s, ctxt, p_s, grad, x_s, dmid_s, gt_s, bias_s,
-    small, small_z,
+    dattn, h1t, dh1, dqkv, watt, qkv_s, dc_s, ctx_s, ctxt, p_s, grad, x_s, dmid_s, gt_s, bias_s,
+    small, small_line,
     r0, r1a, r1b, r2, r3, rs_send, rs_recv, sm_send, sm_recv,
     in_sem, ctx_sem, tile_sem, dmid_sem, gt_sem,
 ):
@@ -895,9 +924,9 @@
     rows = images * seq
     block = rows // 7
     model = x_s.shape[1]
-    pair = 2
-    tr = pair * sp
-    tiles = images // pair
+    quad = 4
+    tr = quad * sp
+    tiles = images // quad
     at = Place()
     dmid_in = pltpu.make_async_copy(dmid_hbm, dh1, in_sem.at[0])
     watt_copy = pltpu.make_async_copy(watt_hbm, watt, in_sem.at[1])
@@ -909,10 +938,10 @@
         return pltpu.make_async_copy(dmid_hbm.at[:, r], dmid_s.at[lax.rem(i, 2)], dmid_sem.at[lax.rem(i, 2)])
 
     def ctx_copy(g):
-        return pltpu.make_async_copy(ctx_hbm.at[g], ctx_s.at[lax.rem(g, 2)], ctx_sem.at[lax.rem(g, 2)])
+        return pltpu.make_async_copy(ctx_hbm.at[g], ctx_s, ctx_sem.at[0])
 
     def tile_copies(g, i):
-        r, im = pl.ds(pl.multiple_of(i * tr, 16), tr), pl.ds(i * pair, pair)
+        r, im = pl.ds(pl.multiple_of(i * tr, 16), tr), pl.ds(i * quad, quad)
         return [
             pltpu.make_async_copy(qkv_hbm.at[g, r], qkv_s.at[r], tile_sem.at[0, i]),
             pltpu.make_async_copy(p_hbm.at[g, im], p_s.at[im], tile_sem.at[1, i]),
@@ -934,19 +963,18 @@
     for g in range(groups):
         scatter.append(
             scatter_both(
-                at, held + g, (grad.at[(held + g) % 2, 0], grad.at[(held + g) % 2, 1]), scratch, (gatt_ref.at[g, 0], gatt_ref.at[g, 1])
+                at, held + g, (grad.at[g % held, 0], grad.at[g % held, 1]), scratch, (gatt_ref.at[g, 0], gatt_ref.at[g, 1])
             )
         )
-    own_z = small_z.at[at.z]
-    sm = [
-        remote(small.at[0], small.at[1], sm_send.at[0], sm_recv.at[0], at.sib),
-        remote(small.at[2], small.at[3], sm_send.at[1], sm_recv.at[1], at.peer_x),
-        remote(small.at[4], small.at[5], sm_send.at[2], sm_recv.at[2], at.peer_y),
+    own_quad, own_line = small.at[at.quad], small_line.at[at.line]
+    sm_quad = [remote(own_quad, own_quad, sm_send.at[k], sm_recv.at[k], d) for k, d in enumerate(at.quad_peers)]
+    sm_line = [
+        remote(own_line, own_line, sm_send.at[3 + k], sm_recv.at[3 + k], d) for k, d in enumerate(at.line_peers)
     ]
-    sm_z = [remote(own_z, own_z, sm_send.at[3 + d], sm_recv.at[3 + d], at.peers_z[d]) for d in range(NZ - 1)]
-    at.barrier()
-    late_copies[0].wait()
-    scatter[0][0]()
+    at.barrier(at.quad_peers + at.line_peers)
+    for k in range(held):
+        late_copies[k].wait()
+        scatter[k][0]()
 
     dmid_in.wait()
 
@@ -968,90 +996,102 @@
 
     def by_image(i, _):
         h = pad_rows(load_columns(dh1, pl.ds(i, seq, stride=images)), sp)
-        dqkv[pl.ds(pl.multiple_of(i * sp, 16), sp), :] = h.astype(BF16)
+        dqkv[0, pl.ds(pl.multiple_of(i * sp, 16), sp), :] = h.astype(BF16)
         return 0
 
     lax.fori_loop(0, images, by_image, 0)
+
+    for k in range(held):
+        scatter[k][1]()
 
     def turn(j, _):
         r = pl.ds(pl.multiple_of(j * 128, 128), 128)
-        h1t[:, r] = dqkv[r, :].T
+        h1t[:, r] = dqkv[0, r, :].T
         return 0
 
     lax.fori_loop(0, images * sp // 128, turn, 0)
-    dh1[...] = jnp.zeros(dh1.shape, F32)
     watt_copy.wait()
-    wait_all(late_copies[1:])
-
-    entries = [(s, scatter[0][k]) for k, s in ((1, 0), (2, 2), (3, 4), (4, 7))]
-    for j in range(1, held):
-        entries += [(2 + s, scatter[j][k]) for k, s in enumerate((0, 2, 4, 6, 9))]
-    for g in range(groups - 1):
-        entries += [(6 * (g + 1) + s, scatter[held + g][k]) for k, s in enumerate((0, 1, 3, 5, 7))]
-    last = scatter[held + groups - 1]
+
+    entries = []
+    for k, slots in enumerate(((2, 8, 12), (4, 10, 14), (8, 11, 16))):
+        entries += [(n, scatter[k][2 + j]) for j, n in enumerate(slots)]
+    for g, slots in enumerate(((12, 15, 18, 21, 27), (14, 16, 20, 22, 30), (18, 20, 26, 30, 31))):
+        entries += [(n, scatter[held + g][j]) for j, n in enumerate(slots)]
     entries.sort(key=lambda e: e[0])
+
+    def spot(n):
+        return (n % 2, (n // 6, n % 6 // 2)) if n % 6 < 4 else (n % 6, (n // 6,))
+
+    tail_at = 6 * groups
     plan = planned(
-        [("tile" if s % 6 < 4 else s % 6, (s // 6, s % 6) if s % 6 < 4 else (s // 6,), step)
-         for s, step in entries if s < 6 * groups]
-    )
-    tail = [step for s, step in entries if s >= 6 * groups]
+        [spot(n) + (step,) for n, step in entries if n < tail_at]
+        + [("through", (n - tail_at,), step) for n, step in entries if tail_at <= n < tail_at + 4]
+        + [("norm", (n - tail_at - 4,), step) for n, step in entries if tail_at + 4 <= n < tail_at + 11]
+    )
+    tail = [[step for n, step in entries if n == at_end] for at_end in (tail_at + 12, tail_at + 13)]
 
     left = left_half(sp)
     scale = HEAD_DIM ** (-0.5)
 
+    units = [(a, t) for a in range(quad) for t in range(NTP)]
+
     def group(g, _):
+        keep = lax.rem(g, grad.shape[0])
+        ctx_copy(g).wait()
+        ctxt[...] = ctx_s[...].T
         pl.when(g + 1 < groups)(lambda: ctx_copy(g + 1).start())
-        slot = lax.rem(g, 2)
-        keep = lax.rem(held + g, 2)
 
         def tile(i, acc):
             wait_all(tile_copies(g, i))
-            run_slot(plan, "tile", (g, i))
+            run_slot(plan, 0, (g, i))
             r = pl.ds(pl.multiple_of(i * tr, 16), tr)
-            wa, wb = matrix(watt.at[g, 0]), matrix(watt.at[g, 1])
-            dc = dot(dattn[r, :], out_columns(wb), 1, 0).astype(BF16)
-            qkv = qkv_s[r, :]
-            blocks = []
-            for a in range(pair):
-                part = qkv[a * sp : (a + 1) * sp]
-                dqs, dks, dvs = [], [], []
-                for t in range(NTP):
-                    q = part[:, t * HALF : t * HALF + 128] * jnp.asarray(scale, BF16)
-                    k = part[:, t * HALF + 128 : t * HALF + HALF]
-                    v = part[:, 2 * HALF + t * 128 : 2 * HALF + t * 128 + 128]
-                    dcx = dc[a * sp : (a + 1) * sp, t * 128 : (t + 1) * 128]
-                    dp = dot(split_heads(v, left), dcx, 1, 1)
-                    kt = k.T
-                    dqt, ds, ps = [], [], []
-                    for h in range(2):
-                        low = p_s[i * pair + a, t, h][:, :sp]
-                        p = low.astype(F32)
-                        pd = p * dp[h * sp : (h + 1) * sp]
-                        s = (pd - p * jnp.sum(pd, axis=0, keepdims=True)).astype(BF16)
-                        ds.append(s)
-                        ps.append(low)
-                        dqt.append(dot(kt[h * HEAD_DIM : (h + 1) * HEAD_DIM], s, 1, 0))
-                    dqs.append(jnp.concatenate(dqt, axis=0).T * scale)
-                    dk = dot(jnp.concatenate(ds, axis=0), q, 1, 0)
-                    dks.append(jnp.where(left, dk[:sp], dk[sp:]))
-                    dv = dot(jnp.concatenate(ps, axis=0), dcx, 1, 0)
-                    dvs.append(jnp.where(left, dv[:sp], dv[sp:]))
-                blocks.append(jnp.concatenate([dqs[0], dks[0], dqs[1], dks[1], dvs[0], dvs[1]], axis=1))
-            d = jnp.concatenate(blocks, axis=0).astype(BF16)
-            dqkv[r, :] = d
-            back = dot(d, projection(wa, wb), 1, 1)
-            for a in range(pair):
-                mine = pl.ds(i * pair + a, seq, stride=images)
-                store_columns(dh1, mine, load_columns(dh1, mine) + back[a * sp : a * sp + seq])
+            dc_s[...] = dot(dattn[r, :], out_columns(matrix(watt.at[g, 1])), 1, 0).astype(BF16)
+            run_slot(plan, 1, (g, i))
+            qkv, dc = qkv_s[r, :], dc_s[...]
+
+            def cut(a, first):
+                return qkv[a * sp : (a + 1) * sp, first : first + 128]
+
+            def wide(v):
+                return pad_rows(v, LANES)
+
+            def grads_in(a, t):
+                return wide(dc[a * sp : (a + 1) * sp, t * 128 : (t + 1) * 128])
+
+            dps = [dot(split_heads(cut(a, 2 * HALF + t * 128), left), grads_in(a, t), 1, 1) for a, t in units]
+            dss = []
+            for (a, t), dp in zip(units, dps):
+                ds = []
+                for h in range(2):
+                    p = p_s[i * quad + a, t, h].astype(F32)
+                    pd = p * dp[h * sp : (h + 1) * sp]
+                    ds.append((pd - p * jnp.sum(pd, axis=0, keepdims=True)).astype(BF16))
+                dss.append(ds)
+            parts = []
+            for (a, t), ds in zip(units, dss):
+                q = wide(cut(a, t * HALF) * jnp.asarray(scale, BF16))
+                kt = cut(a, t * HALF + 128).T
+                dqt = [dot(kt[h * HEAD_DIM : (h + 1) * HEAD_DIM], ds[h], 1, 0) for h in range(2)]
+                dk = dot(jnp.concatenate(ds, axis=0), q, 1, 0)
+                ps = jnp.concatenate([p_s[i * quad + a, t, h] for h in range(2)], axis=0)
+                dv = dot(ps, grads_in(a, t), 1, 0)
+                parts.append((
+                    jnp.concatenate(dqt, axis=0).T[:sp] * scale,
+                    jnp.where(left, dk[:sp], dk[sp:]),
+                    jnp.where(left, dv[:sp], dv[sp:]),
+                ))
+            for a in range(quad):
+                (q0, k0, v0), (q1, k1, v1) = parts[NTP * a], parts[NTP * a + 1]
+                d = jnp.concatenate([q0, k0, q1, k1, v0, v1], axis=1).astype(BF16)
+                dqkv[g, pl.ds(pl.multiple_of(i * tr + a * sp, 16), sp), :] = d
+                acc = acc + jnp.sum(d.astype(F32), axis=0, keepdims=True)
             pl.when(g + 1 < groups)(lambda: start_all(tile_copies(g + 1, i)))
-            return acc + jnp.sum(d.astype(F32), axis=0, keepdims=True)
-
-        ctx_copy(g).wait()
-        ctxt[...] = ctx_s[slot].T
-        bias_s[g] = lax.fori_loop(0, images // pair, tile, jnp.zeros((1, model), F32))
+            return acc
+
+        bias_s[g] = lax.fori_loop(0, tiles, tile, jnp.zeros((1, model), F32))
         run_slot(plan, 4, (g,))
         shape = grad.shape[2:]
-        gw = dot(h1t[...], dqkv[...], 1, 0).astype(BF16)
+        gw = dot(h1t[...], dqkv[g], 1, 0).astype(BF16)
         grad[keep, 0] = gw[:, : 2 * HALF].reshape(shape)
         run_slot(plan, 5, (g,))
         go = dot(ctxt[...], dattn[...], 1, 0).T.astype(BF16)
@@ -1061,61 +1101,71 @@
         return 0
 
     lax.fori_loop(0, groups, group, 0)
-    last[0]()
     dmid_copy(0).start()
+    small_tr = 2 * sp
+
+    def through(i, _):
+        run_slot(plan, "through", (i,))
+        r = pl.ds(pl.multiple_of(i * small_tr, 16), small_tr)
+        d = jnp.concatenate([dqkv[g, r, :] for g in range(groups)], axis=1)
+        w = jnp.concatenate(
+            [projection(matrix(watt.at[g, 0]), matrix(watt.at[g, 1])) for g in range(groups)], axis=1
+        )
+        back = dot(d, w, 1, 1)
+        for a in range(2):
+            store_columns(dh1, pl.ds(i * 2 + a, seq, stride=images), back[a * sp : a * sp + seq])
+        return 0
+
+    lax.fori_loop(0, images // 2, through, 0)
+
+    def gt_copy(i):
+        r = pl.ds(pl.multiple_of(i * block, 16), block)
+        return pltpu.make_async_copy(gt_s.at[lax.rem(i, 2)], gt_hbm.at[r], gt_sem.at[lax.rem(i, 2)])
 
     def first_norm_back(i, acc):
+        run_slot(plan, "norm", (i,))
+        pl.when(i >= 2)(lambda: gt_copy(i - 2).wait())
         pl.when(i + 1 < 7)(lambda: dmid_copy(i + 1).start())
         dmid_copy(i).wait()
         r = pl.ds(pl.multiple_of(i * block, 16), block)
         xhat, rstd = normed(x_s[r, :].astype(F32))
         e = load_columns(dh1, r)
         d = load_columns(dmid_s.at[lax.rem(i, 2)], slice(None))
-        gt_s[i] = d + norm_back(e, norm_ref[0:1, :], xhat, rstd)
-        pltpu.make_async_copy(gt_s.at[i], gt_hbm.at[r], gt_sem.at[i]).start()
+        gt_s[lax.rem(i, 2)] = d + norm_back(e, norm_ref[0:1, :], xhat, rstd)
+        gt_copy(i).start()
         return (acc[0] + jnp.sum(e * xhat, axis=0, keepdims=True), acc[1] + jnp.sum(e, axis=0, keepdims=True))
 
     zero = jnp.zeros((1, model), F32)
-    acc = lax.fori_loop(0, 4, first_norm_back, (zero, zero))
-    for step in tail:
-        step()
-    last[1]()
-    acc = lax.fori_loop(4, 7, first_norm_back, acc)
-    small[0] = jnp.zeros(small.shape[1:], F32)
-    small[0, 0:1, :] = acc[0]
-    small[0, 1:2, :] = acc[1]
-    small[0, 2:6, :] = sums_ref[0:4, :]
+    acc = lax.fori_loop(0, 7, first_norm_back, (zero, zero))
+    own_quad[...] = jnp.zeros(own_quad.shape, F32)
+    own_quad[0:1, :] = acc[0]
+    own_quad[1:2, :] = acc[1]
+    own_quad[2:6, :] = sums_ref[0:4, :]
     own_cols = groups * 128
     for g in range(groups):
         for t in range(NTP):
             cols = slice(t * own_cols + 128 * g, t * own_cols + 128 * g + 128)
-            small[0, 6:7, cols] = bias_s[g, :, t * HALF : t * HALF + 128]
-            small[0, 7:8, cols] = bias_s[g, :, 2 * HALF + t * 128 : 2 * HALF + t * 128 + 128]
+            own_quad[6:7, cols] = bias_s[g, :, t * HALF : t * HALF + 128]
+            own_quad[7:8, cols] = bias_s[g, :, 2 * HALF + t * 128 : 2 * HALF + t * 128 + 128]
     for f in range(chunks):
         for t in range(NTP):
             first = t * chunks * HALF + f * HALF
             row, col = 8 + first // model, first % model
-            small[0, row : row + 1, col : col + HALF] = b1g_ref[f, :, t * HALF : t * HALF + HALF]
-    sm[0].start()
-    last[2]()
-    sm[0].wait()
-    small[2] = small[0] + small[1]
-    sm[1].start()
-    last[3]()
-    sm[1].wait()
-    small[4] = small[2] + small[3]
-    sm[2].start()
-    last[4]()
-    sm[2].wait()
-    small_z[at.z] = small[4] + small[5]
-    start_all(sm_z)
-    for i in range(7):
-        r = pl.ds(i * block, block)
-        pltpu.make_async_copy(gt_s.at[i], gt_hbm.at[r], gt_sem.at[i]).wait()
-    wait_all(sm_z)
-    total = small_z[0]
-    for k in range(1, NZ):
-        total = total + small_z[k]
+            own_quad[row : row + 1, col : col + HALF] = b1g_ref[f, :, t * HALF : t * HALF + HALF]
+    start_all(sm_quad)
+    for step in tail[0]:
+        step()
+    wait_all(sm_quad)
+    own_line[...] = (small[0] + small[1]) + (small[2] + small[3])
+    start_all(sm_line)
+    for step in tail[1]:
+        step()
+    gt_copy(5).wait()
+    gt_copy(6).wait()
+    wait_all(sm_line)
+    total = small_line[0]
+    for k in range(1, NZ * NY):
+        total = total + small_line[k]
     small_ref[...] = total
 
 
@@ -1179,7 +1229,7 @@
     own_rows, own_cols = w_qkv.shape[1], w_qkv.shape[2]
     groups = own_cols // 128
     chunks = w_fc1.shape[1] // HALF
-    early, summed = 2, chunks - 2
+    early, summed = 2, chunks - 3
     held = chunks - summed
     wide = NTP * HALF
     cube = (NZ, NY, NCORE, own_rows, wide)
@@ -1189,7 +1239,7 @@
     def params(k):
         return pltpu.CompilerParams(collective_id=k, has_side_effects=True, vmem_limit_bytes=VMEM_BYTES)
 
-    n_ag = groups + early
+    n_ag = groups + early + 2
     flat_rows = images * seq
 
     def by_token(a):
@@ -1259,16 +1309,17 @@
         ],
         scratch_shapes=[
             pltpu.VMEM((rows, model), BF16), pltpu.VMEM((model, rows), BF16),
-            pltpu.VMEM((model // 128, flat_rows, 128), F32), pltpu.VMEM((rows, model), BF16),
+            pltpu.VMEM((model // 128, flat_rows, 128), F32), pltpu.VMEM((groups, rows, model), BF16),
             pltpu.VMEM((groups, 2) + cube, BF16),
-            pltpu.VMEM((rows, model), BF16), pltpu.VMEM((2, rows, HALF), BF16), pltpu.VMEM((HALF, rows), BF16),
-            pltpu.VMEM((images, NTP, 2, sp, LANES), BF16), pltpu.VMEM((2, 2) + cube, BF16),
+            pltpu.VMEM((rows, model), BF16), pltpu.VMEM((4 * sp, HALF), BF16),
+            pltpu.VMEM((rows, HALF), BF16), pltpu.VMEM((HALF, rows), BF16),
+            pltpu.VMEM((images, NTP, 2, sp, LANES), BF16), pltpu.VMEM((held, 2) + cube, BF16),
             pltpu.VMEM((flat_rows, model), BF16), pltpu.VMEM((2, model // 128, flat_rows // 7, 128), F32),
-            pltpu.VMEM((7, flat_rows // 7, model), F32), pltpu.VMEM((groups, 1, model), F32),
-            pltpu.VMEM((6, 16, model), F32), pltpu.VMEM((NZ, 16, model), F32),
+            pltpu.VMEM((2, flat_rows // 7, model), F32), pltpu.VMEM((groups, 1, model), F32),
+            pltpu.VMEM((4, 16, model), F32), pltpu.VMEM((NZ * NY, 16, model), F32),
         ]
         + scatter_scratch(held + groups, own_rows)
-        + [dma((6,)), dma((6,)), dma((3 + held,)), dma((2,)), dma((2, images // 2)), dma((2,)), dma((8,))],
+        + [dma((10,)), dma((10,)), dma((3 + held,)), dma((1,)), dma((2, 2)), dma((2,)), dma((2,))],
         compiler_params=params(2),
     )(norm_params, sums, b1g, x_rows, dmid, grad_late, watt, qkv, ctx, p)
 

time: 266 us -> 239 us (0.90)
  Pallas kernels: 259 us -> 229 us
    pallas_call x1, Pallas kernels: 97.9 us -> 79.7 us  [fused_device(): pl.pallas_call(functools.partial(feed_forward_kernel, (images, seq, sp, c...]
    pallas_call x1, Pallas kernels: 87.4 us -> 80.3 us  [fused_device(): pl.pallas_call(functools.partial(attention_back_kernel, (images, seq, sp,...]
    pallas_call x1, Pallas kernels: 69 us -> 64.8 us  [fused_device(): pl.pallas_call(functools.partial(attention_kernel, (images, seq, sp, grou...]
where the time goes in v2:
time: 239 us; the launch traced here: 236 us
  Pallas kernels  229 us (96%)
  local copies, waits for them, and re-layouts  5.7 us (2%)
    pallas_call x1, Pallas kernels, fused_device(): pl.pallas_call(functools.partial(attention_back_kernel, (images, seq, sp,...  80.3 us
    pallas_call x1, Pallas kernels, fused_device(): pl.pallas_call(functools.partial(feed_forward_kernel, (images, seq, sp, c...  79.7 us
    pallas_call x1, Pallas kernels, fused_device(): pl.pallas_call(functools.partial(attention_kernel, (images, seq, sp, grou...  64.8 us
    unnamed x4, local copies, waits for them, and re-layouts  5.7 us

profile of v2, /device:TPU:0, one launch (start us, length us, event | category | flops | bytes accessed | tf_op | source)
XLA Modules:
  0.0 236.3 jit_solution(13298499165861052321)
XLA Ops:
  1.3 64.8 %attention.1 = (bf16[3,1664,768]{2,1,0:T(8,128)(2,1)}, bf16[3,1664,256]{2,1,0:T(8,128)(2,1)}, f32[6,1568,128]{2,1,0:T(8,128)}, bf16[3,8,2,2,208,256]{5,4,3,2,1,0...) custom-call(bf16[1568,768]{1,0:T(8,128)(2,1)} %bitcast.33, ...), custom_call_target="tpu_custom_call" | custom-call | tf_op jit(solution)/shard_map/attention/pallas_call | solution.py:1252
  66.2 79.7 %feed_forward.1 = (bf16[1568,768]{1,0:T(8,128)(2,1)}, f32[6,1568,128]{2,1,0:T(8,128)}, bf16[3,2,4,2,2,48,512]{6,5,4,3,2,1,0:T(8,128)(2,1)}, f32[8,768]{1,0:T(8,1...) custom-call(s32[1]{0:T(128)S(6)} %copy.63.counts_ref, f32[4,768]{1,0:T(4,128)} %refs_4_.1, f32[2,768]{1,0:T(2,128)} %refs_11_.1, ...), custom_call_target="tpu_custom_call" | custom-call | tf_op jit(solution)/shard_map/feed_forward/pallas_call | solution.py:1275
  145.8 80.3 %attention_back.1 = (f32[1568,768]{1,0:T(8,128)}, f32[3,2,48,256]{3,2,1,0:T(8,128)}, f32[3,2,48,256]{3,2,1,0:T(8,128)}, f32[16,768]{1,0:T(8,128)}) custom-call(f32[4,768]{1,0:T(4,128)} %refs_4_.1, f32[8,768]{1,0:T(8,128)} %get-tuple-element.89.sums_ref, f32[6,1,512]{2,1,0:T(1,128)} %get-tuple-element.90.b1g_ref, bf16[1568,768]{1,0:T(8,128)(2,1)} %bitcast.34, ...), custom_call_target="tpu_custom_call" | custom-call | tf_op jit(solution)/shard_map/attention_back/pallas_call | solution.py:1301
  226.2 4.4 %adamw_step.1 = (f32[4,768]{1,0:T(4,128)}, f32[3,48,384]{2,1,0:T(8,128)}, f32[2,24]{1,0:T(2,128)}, f32[48,384]{1,0:T(8,128)}, f32[48,1536]{1,0:T(8,128)}, /*inde...) custom-call(f32[3,2,48,256]{3,2,1,0:T(8,128)} %get-tuple-element.98., ...), custom_call_target="tpu_custom_call" | custom-call | tf_op jit(solution)/shard_map/adamw_step/pallas_call | solution.py:1334
  230.6 0.0 copy-start
  230.6 3.4 %copy.64 = bf16[8,196,768]{2,0,1:T(8,128)(2,1)} copy(bf16[8,196,768]{2,0,1:T(8,128)(2,1)} %bitcast.36) | data formatting | bytes 4816896
  234.0 0.1 copy-done
  234.0 2.2 copy.65
Async XLA Ops:
  230.6 3.5 %copy-start = (f32[1568,768]{1,0:T(8,128)S(1)}, f32[1568,768]{1,0:T(8,128)}, u32[]{:S(2)}) copy-start(f32[1568,768]{1,0:T(8,128)} %get-tuple-element.97) | copy-start | bytes 14450692

commit v3 on v2

--- a/solution.py
+++ b/solution.py
@@ -595,6 +595,7 @@
     head_step(0)
     start_all(bias_steps[0])
     steps[1][0]()
+    steps[2][0]()
     for f in range(chunks - groups):
         cols = slice(HALF * f, HALF * f + HALF)
         own[groups + f, 0] = wfc1_ref[:, cols].astype(BF16)
@@ -619,7 +620,6 @@
     head_step(1)
     wait_all(bias_steps[0])
     start_all(bias_steps[1])
-    steps[2][0]()
     lax.fori_loop(0, 7, first_norm, 0)
     head_step(2)
     wait_all(bias_steps[1])
@@ -651,9 +651,10 @@
         )
     head_step(4)
 
-    when = {1: [None, None, 2, 4, 4], 2: [None, 2, 4, 8, 8]}
-    when.update({groups + f: ns for f, ns in enumerate([[0, 4, 7, 10, 13], [4, 8, 11, 14, 14]])})
-    entries = sorted((n, k, k_step) for k, ns in when.items() for k_step, n in enumerate(ns) if n is not None)
+    when = {1: [None, None, 1, 4.1, 4.2], 2: [None, 2, 4, 7, 8]}
+    when.update({groups + f: ns for f, ns in enumerate([[1.5, 5, 8.5, 11, 14], [5, 9, 12, 14.1, 14.2]])})
+    entries = sorted((n, k, j) for k, ns in when.items() for j, n in enumerate(ns) if n is not None)
+    entries = [(int(n), k, j) for n, k, j in entries]
     last = 4 * groups + 2
     plan = planned(
         [("out", (n - 4 * groups,), steps[k][j]) if n >= 4 * groups else (n % 2, (n // 4, n % 4 // 2), steps[k][j])
@@ -773,9 +774,10 @@
 
     def mid_copy(i):
         r = pl.ds(pl.multiple_of(i * block, 16), block)
-        return pltpu.make_async_copy(mid_hbm.at[:, r], mid_s.at[lax.rem(i, 3)], mid_sem.at[lax.rem(i, 3)])
+        return pltpu.make_async_copy(mid_hbm.at[:, r], mid_s.at[lax.rem(i, 4)], mid_sem.at[lax.rem(i, 4)])
 
     mid_copy(0).start()
+    mid_copy(1).start()
     start_all(w_copies)
     late = chunks - early
     gather = {
@@ -803,10 +805,10 @@
     live = jnp.where(image < count, 1.0, 0.0).astype(F32)
 
     def second_norm(i, _):
-        pl.when(i + 1 < 7)(lambda: mid_copy(i + 1).start())
+        pl.when(i + 2 < 7)(lambda: mid_copy(i + 2).start())
         mid_copy(i).wait()
         r = pl.ds(pl.multiple_of(i * block, 16), block)
-        xhat, _r = normed(load_columns(mid_s.at[lax.rem(i, 3)], slice(None)))
+        xhat, _r = normed(load_columns(mid_s.at[lax.rem(i, 4)], slice(None)))
         h2[r, :] = (xhat * norm_ref[2:3, :] + norm_ref[3:4, :]).astype(BF16)
         dm[r, :] = (dm[r, :].astype(F32) * live).astype(BF16)
         mlp[r, :] = jnp.zeros((block, mlp.shape[1]), F32)
@@ -870,25 +872,26 @@
             pl.when(f == k)(late_copy(k).start)
         return 0
 
+    mid_copy(0).start()
+    mid_copy(1).start()
     lax.fori_loop(0, chunks, chunk, 0)
-    mid_copy(0).start()
 
     def dmid_copy(i):
         r = pl.ds(pl.multiple_of(i * block, 16), block)
-        return pltpu.make_async_copy(mid_s.at[lax.rem(i, 3)], dmid_hbm.at[:, r], out_sem.at[16 + lax.rem(i, 3)])
+        return pltpu.make_async_copy(mid_s.at[lax.rem(i, 4)], dmid_hbm.at[:, r], out_sem.at[16 + lax.rem(i, 4)])
 
     def second_norm_back(i, acc):
         pl.when(i >= 2)(lambda: dmid_copy(i - 2).wait())
-        pl.when(i + 1 < 7)(lambda: mid_copy(i + 1).start())
+        pl.when(i + 2 < 7)(lambda: mid_copy(i + 2).start())
         mid_copy(i).wait()
         r = pl.ds(pl.multiple_of(i * block, 16), block)
-        mid = load_columns(mid_s.at[lax.rem(i, 3)], slice(None))
+        mid = load_columns(mid_s.at[lax.rem(i, 4)], slice(None))
         xhat, rstd = normed(mid)
         h2[r, :] = (mid + mlp[r, :] + bout_ref[1:2, :]).astype(BF16)
         e = dh2[r, :]
         live = dm[r, :].astype(F32)
         d = live + norm_back(e, norm_ref[2:3, :], xhat, rstd)
-        store_columns(mid_s.at[lax.rem(i, 3)], slice(None), d)
+        store_columns(mid_s.at[lax.rem(i, 4)], slice(None), d)
         pltpu.make_async_copy(h2.at[r], bo_hbm.at[r], out_sem.at[8 + i]).start()
         dmid_copy(i).start()
         terms = (e * xhat, e, d, live)
@@ -935,7 +938,7 @@
 
     def dmid_copy(i):
         r = pl.ds(pl.multiple_of(i * block, 16), block)
-        return pltpu.make_async_copy(dmid_hbm.at[:, r], dmid_s.at[lax.rem(i, 2)], dmid_sem.at[lax.rem(i, 2)])
+        return pltpu.make_async_copy(dmid_hbm.at[:, r], dmid_s.at[lax.rem(i, 3)], dmid_sem.at[lax.rem(i, 3)])
 
     def ctx_copy(g):
         return pltpu.make_async_copy(ctx_hbm.at[g], ctx_s, ctx_sem.at[0])
@@ -1001,8 +1004,7 @@
 
     lax.fori_loop(0, images, by_image, 0)
 
-    for k in range(held):
-        scatter[k][1]()
+    scatter[0][1]()
 
     def turn(j, _):
         r = pl.ds(pl.multiple_of(j * 128, 128), 128)
@@ -1013,8 +1015,8 @@
     watt_copy.wait()
 
     entries = []
-    for k, slots in enumerate(((2, 8, 12), (4, 10, 14), (8, 11, 16))):
-        entries += [(n, scatter[k][2 + j]) for j, n in enumerate(slots)]
+    for k, slots in enumerate(((2, 8, 12), (2, 6, 10, 14), (5, 9, 12, 16))):
+        entries += [(n, scatter[k][5 - len(slots) + j]) for j, n in enumerate(slots)]
     for g, slots in enumerate(((12, 15, 18, 21, 27), (14, 16, 20, 22, 30), (18, 20, 26, 30, 31))):
         entries += [(n, scatter[held + g][j]) for j, n in enumerate(slots)]
     entries.sort(key=lambda e: e[0])
@@ -1100,8 +1102,9 @@
         ).reshape(shape)
         return 0
 
+    dmid_copy(0).start()
+    dmid_copy(1).start()
     lax.fori_loop(0, groups, group, 0)
-    dmid_copy(0).start()
     small_tr = 2 * sp
 
     def through(i, _):
@@ -1125,12 +1128,12 @@
     def first_norm_back(i, acc):
         run_slot(plan, "norm", (i,))
         pl.when(i >= 2)(lambda: gt_copy(i - 2).wait())
-        pl.when(i + 1 < 7)(lambda: dmid_copy(i + 1).start())
+        pl.when(i + 2 < 7)(lambda: dmid_copy(i + 2).start())
         dmid_copy(i).wait()
         r = pl.ds(pl.multiple_of(i * block, 16), block)
         xhat, rstd = normed(x_s[r, :].astype(F32))
         e = load_columns(dh1, r)
-        d = load_columns(dmid_s.at[lax.rem(i, 2)], slice(None))
+        d = load_columns(dmid_s.at[lax.rem(i, 3)], slice(None))
         gt_s[lax.rem(i, 2)] = d + norm_back(e, norm_ref[0:1, :], xhat, rstd)
         gt_copy(i).start()
         return (acc[0] + jnp.sum(e * xhat, axis=0, keepdims=True), acc[1] + jnp.sum(e, axis=0, keepdims=True))
@@ -1172,11 +1175,28 @@
 def step_kernel(dims, *refs):
     groups, chunks, held = dims
     names = ("norm", "qkv", "bqv", "out", "fc1", "bfc1", "fc2", "bout")
-    gff_ref, glate_ref, gatt_ref, small_ref = refs[:4]
+    bo_hbm, gt_hbm, gff_ref, glate_ref, gatt_ref, small_ref = refs[:6]
     n = len(names)
-    ps, ms, vs = (dict(zip(names, refs[4 + k * n : 4 + (k + 1) * n])) for k in range(3))
-    outs = refs[4 + 3 * n :]
-    g_out, u_out, m_out, v_out = (dict(zip(names, outs[k * n : (k + 1) * n])) for k in range(4))
+    ps, ms, vs = (dict(zip(names, refs[6 + k * n : 6 + (k + 1) * n])) for k in range(3))
+    outs = refs[6 + 3 * n :]
+    bo_out, gt_out = outs[:2]
+    g_out, u_out, m_out, v_out = (dict(zip(names, outs[2 + k * n : 2 + (k + 1) * n])) for k in range(4))
+    bo_s, gt_s, sem = outs[2 + 4 * n :]
+    pieces = 7
+    block = bo_s.shape[0] // pieces
+    moves = []
+    for j in range(pieces):
+        r = pl.ds(j * block, block)
+        for k, (src, mid, dst) in enumerate(((gt_hbm, gt_s, gt_out), (bo_hbm, bo_s, bo_out))):
+            moves.append((
+                pltpu.make_async_copy(src.at[r], mid.at[r], sem.at[0, k, j]),
+                pltpu.make_async_copy(mid.at[r], dst.at[r], sem.at[1, k, j]),
+            ))
+    for first, _second in moves:
+        first.start()
+    for first, second in moves:
+        first.wait()
+        second.start()
     late = chunks - held
 
     def ff(f, h):
@@ -1212,6 +1232,8 @@
     turned = pltpu.roll(small_ref[8:16, :], lax.rem(model - lax.rem(part, per) * width, model), 1)[:, :width]
     at_row = lax.broadcasted_iota(jnp.int32, turned.shape, 0)
     update("bfc1", ..., jnp.sum(jnp.where(at_row == part // per, turned, 0.0), axis=0, keepdims=True))
+    for _first, second in moves:
+        second.wait()
 
 
 def sds(shape, dtype):
@@ -1288,11 +1310,11 @@
             pltpu.VMEM((rows, model), BF16), pltpu.VMEM((model, rows), BF16),
             pltpu.VMEM((flat_rows, model), F32), pltpu.VMEM((flat_rows, model), F32),
             pltpu.VMEM((rows, wide), BF16), pltpu.VMEM((rows, wide), BF16),
-            pltpu.VMEM((2, 2) + cube, BF16), pltpu.VMEM((3, model // 128, flat_rows // 7, 128), F32),
+            pltpu.VMEM((2, 2) + cube, BF16), pltpu.VMEM((4, model // 128, flat_rows // 7, 128), F32),
         ]
         + scatter_scratch(summed, own_rows)
         + [
-            dma((late, 2, AG_SEMS)), dma((late, 2, AG_SEMS)), dma((late, 2)), dma((2 + early,)), dma((3,)),
+            dma((late, 2, AG_SEMS)), dma((late, 2, AG_SEMS)), dma((late, 2)), dma((2 + early,)), dma((4,)),
             dma((24,)),
         ],
         compiler_params=params(1),
@@ -1314,12 +1336,12 @@
             pltpu.VMEM((rows, model), BF16), pltpu.VMEM((4 * sp, HALF), BF16),
             pltpu.VMEM((rows, HALF), BF16), pltpu.VMEM((HALF, rows), BF16),
             pltpu.VMEM((images, NTP, 2, sp, LANES), BF16), pltpu.VMEM((held, 2) + cube, BF16),
-            pltpu.VMEM((flat_rows, model), BF16), pltpu.VMEM((2, model // 128, flat_rows // 7, 128), F32),
+            pltpu.VMEM((flat_rows, model), BF16), pltpu.VMEM((3, model // 128, flat_rows // 7, 128), F32),
             pltpu.VMEM((2, flat_rows // 7, model), F32), pltpu.VMEM((groups, 1, model), F32),
             pltpu.VMEM((4, 16, model), F32), pltpu.VMEM((NZ * NY, 16, model), F32),
         ]
         + scatter_scratch(held + groups, own_rows)
-        + [dma((10,)), dma((10,)), dma((3 + held,)), dma((1,)), dma((2, 2)), dma((2,)), dma((2,))],
+        + [dma((10,)), dma((10,)), dma((3 + held,)), dma((1,)), dma((2, 2)), dma((3,)), dma((2,))],
         compiler_params=params(2),
     )(norm_params, sums, b1g, x_rows, dmid, grad_late, watt, qkv, ctx, p)
 
@@ -1334,11 +1356,13 @@
     outs = pl.pallas_call(
         functools.partial(step_kernel, (groups, chunks, held)),
         name="adamw_step",
-        in_specs=[vm] * 28,
-        out_specs=[vm] * 32,
-        out_shape=shapes * 4,
+        in_specs=[any_] * 2 + [vm] * 28,
+        out_specs=[any_] * 2 + [vm] * 32,
+        out_shape=[sds(bo.shape, BF16), sds(gt.shape, F32)] + shapes * 4,
+        scratch_shapes=[pltpu.VMEM(bo.shape, BF16), pltpu.VMEM(gt.shape, F32), dma((2, 2, 7))],
         compiler_params=pltpu.CompilerParams(vmem_limit_bytes=VMEM_BYTES),
-    )(gff, glate, gatt, small, *weights, *moments)
+    )(bo, gt, gff, glate, gatt, small, *weights, *moments)
+    bo, gt, *outs = outs
     outs = [o.reshape(-1) if k % 8 == 5 else o.T if k % 8 in turned else o for k, o in enumerate(outs)]
     return (by_image(bo), by_image(gt)) + tuple(outs)
 

time: 239 us -> 230 us (0.962)
  local copies, waits for them, and re-layouts: 5.7 us -> 0 us
    pallas_call x1, Pallas kernels: 4.4 us -> 10.2 us  [fused_device(): pl.pallas_call(functools.partial(step_kernel, (groups, chunks, held)), na...]
    unnamed x4 -> x0, local copies, waits for them, and re-layouts: 5.7 us -> none
    pallas_call x1, Pallas kernels: 79.7 us -> 75 us  [fused_device(): pl.pallas_call(functools.partial(feed_forward_kernel, (images, seq, sp, c...]
where the time goes in v3:
time: 230 us; the launch traced here: 229 us
  Pallas kernels  227 us (99%)
    pallas_call x1, Pallas kernels, fused_device(): pl.pallas_call(functools.partial(attention_back_kernel, (images, seq, sp,...  78.2 us
    pallas_call x1, Pallas kernels, fused_device(): pl.pallas_call(functools.partial(feed_forward_kernel, (images, seq, sp, c...  75 us
    pallas_call x1, Pallas kernels, fused_device(): pl.pallas_call(functools.partial(attention_kernel, (images, seq, sp, grou...  63.7 us
    pallas_call x1, Pallas kernels, fused_device(): pl.pallas_call(functools.partial(step_kernel, (groups, chunks, held)), na...  10.2 us

profile of v3, /device:TPU:0, one launch (start us, length us, event | category | flops | bytes accessed | tf_op | source)
XLA Modules:
  0.0 228.6 jit_solution(13558908530635960268)
XLA Ops:
  1.3 63.7 %attention.1 = (bf16[3,1664,768]{2,1,0:T(8,128)(2,1)}, bf16[3,1664,256]{2,1,0:T(8,128)(2,1)}, f32[6,1568,128]{2,1,0:T(8,128)}, bf16[3,8,2,2,208,256]{5,4,3,2,1,0...) custom-call(bf16[1568,768]{1,0:T(8,128)(2,1)} %bitcast.33, ...), custom_call_target="tpu_custom_call" | custom-call | tf_op jit(solution)/shard_map/attention/pallas_call | solution.py:1274
  65.1 75.0 %feed_forward.1 = (bf16[1568,768]{1,0:T(8,128)(2,1)}, f32[6,1568,128]{2,1,0:T(8,128)}, bf16[3,2,4,2,2,48,512]{6,5,4,3,2,1,0:T(8,128)(2,1)}, f32[8,768]{1,0:T(8,1...) custom-call(s32[1]{0:T(128)S(6)} %copy.61.counts_ref, f32[4,768]{1,0:T(4,128)} %refs_6_.1, f32[2,768]{1,0:T(2,128)} %refs_13_.1, ...), custom_call_target="tpu_custom_call" | custom-call | tf_op jit(solution)/shard_map/feed_forward/pallas_call | solution.py:1297
  140.0 78.2 %attention_back.1 = (f32[1568,768]{1,0:T(8,128)}, f32[3,2,48,256]{3,2,1,0:T(8,128)}, f32[3,2,48,256]{3,2,1,0:T(8,128)}, f32[16,768]{1,0:T(8,128)}) custom-call(f32[4,768]{1,0:T(4,128)} %refs_6_.1, f32[8,768]{1,0:T(8,128)} %get-tuple-element.91.sums_ref, f32[6,1,512]{2,1,0:T(1,128)} %get-tuple-element.92.b1g_ref, bf16[1568,768]{1,0:T(8,128)(2,1)} %bitcast.34, ...), custom_call_target="tpu_custom_call" | custom-call | tf_op jit(solution)/shard_map/attention_back/pallas_call | solution.py:1323
  218.2 10.2 %adamw_step.1 = (bf16[1568,768]{1,0:T(8,128)(2,1)}, f32[1568,768]{1,0:T(8,128)}, f32[4,768]{1,0:T(4,128)}, f32[3,48,384]{2,1,0:T(8,128)}, f32[2,24]{1,0:T(2,128)...) custom-call(bf16[1568,768]{1,0:T(8,128)(2,1)} %get-tuple-element.90., ...), custom_call_target="tpu_custom_call" | custom-call | tf_op jit(solution)/shard_map/adamw_step/pallas_call | solution.py:1356

commit v4 on v3

--- a/solution.py
+++ b/solution.py
@@ -931,7 +931,7 @@
     tr = quad * sp
     tiles = images // quad
     at = Place()
-    dmid_in = pltpu.make_async_copy(dmid_hbm, dh1, in_sem.at[0])
+    dmid_in = pltpu.make_async_copy(dmid_hbm, dh1.at[:, pl.ds(0, rows)], in_sem.at[0])
     watt_copy = pltpu.make_async_copy(watt_hbm, watt, in_sem.at[1])
     x_copy = pltpu.make_async_copy(x_hbm, x_s, in_sem.at[2])
     late_copies = [pltpu.make_async_copy(late_hbm.at[k], grad.at[k], in_sem.at[3 + k]) for k in range(held)]
@@ -1263,6 +1263,7 @@
 
     n_ag = groups + early + 2
     flat_rows = images * seq
+    strided_rows = images * (-(-seq // 8) * 8)
 
     def by_token(a):
         return a.transpose(1, 0, 2).reshape(flat_rows, model)
@@ -1284,7 +1285,8 @@
         scratch_shapes=[
             pltpu.VMEM((flat_rows, model), BF16), pltpu.VMEM((rows, model), BF16),
             pltpu.VMEM((groups, rows, model), BF16), pltpu.VMEM((groups, rows, HALF), BF16),
-            pltpu.VMEM((model // 128, flat_rows, 128), F32), pltpu.VMEM((groups, images, NTP, 2, sp, LANES), BF16),
+            pltpu.VMEM((model // 128, strided_rows, 128), F32),
+            pltpu.VMEM((groups, images, NTP, 2, sp, LANES), BF16),
             pltpu.VMEM((groups, 2) + cube, BF16), pltpu.VMEM((groups + chunks, 2, own_rows, HALF), BF16),
             pltpu.VMEM((NTP, NZ, NY, NCORE, 8, 128), F32), pltpu.VMEM((groups, 1, model), F32),
             dma((n_ag, 2, AG_SEMS)), dma((n_ag, 2, AG_SEMS)), dma((n_ag, 2)), dma((6,)), dma((6,)),
@@ -1331,7 +1333,7 @@
         ],
         scratch_shapes=[
             pltpu.VMEM((rows, model), BF16), pltpu.VMEM((model, rows), BF16),
-            pltpu.VMEM((model // 128, flat_rows, 128), F32), pltpu.VMEM((groups, rows, model), BF16),
+            pltpu.VMEM((model // 128, strided_rows, 128), F32), pltpu.VMEM((groups, rows, model), BF16),
             pltpu.VMEM((groups, 2) + cube, BF16),
             pltpu.VMEM((rows, model), BF16), pltpu.VMEM((4 * sp, HALF), BF16),
             pltpu.VMEM((rows, HALF), BF16), pltpu.VMEM((HALF, rows), BF16),

time: 230 us -> 230 us (level)
  no operation moved by 1% of the time
where the time goes in v4:
time: 230 us; the launch traced here: 229 us
  Pallas kernels  227 us (99%)
    pallas_call x1, Pallas kernels, fused_device(): pl.pallas_call(functools.partial(attention_back_kernel, (images, seq, sp,...  78.1 us
    pallas_call x1, Pallas kernels, fused_device(): pl.pallas_call(functools.partial(feed_forward_kernel, (images, seq, sp, c...  75 us
    pallas_call x1, Pallas kernels, fused_device(): pl.pallas_call(functools.partial(attention_kernel, (images, seq, sp, grou...  63.7 us
    pallas_call x1, Pallas kernels, fused_device(): pl.pallas_call(functools.partial(step_kernel, (groups, chunks, held)), na...  10.2 us

profile of v4, /device:TPU:0, one launch (start us, length us, event | category | flops | bytes accessed | tf_op | source)
XLA Modules:
  0.0 228.6 jit_solution(16236682444243435736)
XLA Ops:
  1.3 63.7 %attention.1 = (bf16[3,1664,768]{2,1,0:T(8,128)(2,1)}, bf16[3,1664,256]{2,1,0:T(8,128)(2,1)}, f32[6,1568,128]{2,1,0:T(8,128)}, bf16[3,8,2,2,208,256]{5,4,3,2,1,0...) custom-call(bf16[1568,768]{1,0:T(8,128)(2,1)} %bitcast.33, ...), custom_call_target="tpu_custom_call" | custom-call | tf_op jit(solution)/shard_map/attention/pallas_call | solution.py:1275
  65.1 75.0 %feed_forward.1 = (bf16[1568,768]{1,0:T(8,128)(2,1)}, f32[6,1568,128]{2,1,0:T(8,128)}, bf16[3,2,4,2,2,48,512]{6,5,4,3,2,1,0:T(8,128)(2,1)}, f32[8,768]{1,0:T(8,1...) custom-call(s32[1]{0:T(128)S(6)} %copy.61.counts_ref, f32[4,768]{1,0:T(4,128)} %refs_6_.1, f32[2,768]{1,0:T(2,128)} %refs_13_.1, ...), custom_call_target="tpu_custom_call" | custom-call | tf_op jit(solution)/shard_map/feed_forward/pallas_call | solution.py:1299
  140.0 78.1 %attention_back.1 = (f32[1568,768]{1,0:T(8,128)}, f32[3,2,48,256]{3,2,1,0:T(8,128)}, f32[3,2,48,256]{3,2,1,0:T(8,128)}, f32[16,768]{1,0:T(8,128)}) custom-call(f32[4,768]{1,0:T(4,128)} %refs_6_.1, f32[8,768]{1,0:T(8,128)} %get-tuple-element.91.sums_ref, f32[6,1,512]{2,1,0:T(1,128)} %get-tuple-element.92.b1g_ref, bf16[1568,768]{1,0:T(8,128)(2,1)} %bitcast.34, ...), custom_call_target="tpu_custom_call" | custom-call | tf_op jit(solution)/shard_map/attention_back/pallas_call | solution.py:1325
  218.2 10.2 %adamw_step.1 = (bf16[1568,768]{1,0:T(8,128)(2,1)}, f32[1568,768]{1,0:T(8,128)}, f32[4,768]{1,0:T(4,128)}, f32[3,48,384]{2,1,0:T(8,128)}, f32[2,24]{1,0:T(2,128)...) custom-call(bf16[1568,768]{1,0:T(8,128)(2,1)} %get-tuple-element.90., ...), custom_call_target="tpu_custom_call" | custom-call | tf_op jit(solution)/shard_map/adamw_step/pallas_call | solution.py:1358
